TPU v7x, 256 devices: a whole 4x4x8 slice. The times are simulated.
256 devices in a mesh: section: 8 (over z), seq: 16 (over y, x), head: 2 (over core).
Axes of the slice: x: 4, y: 4, z: 8, core: 2. Of those that a mesh axis runs over, the one named last changes fastest.
Arguments:
- features: bfloat16 [8, 2048, 128, 64], P('section', 'seq', 'head'), may hold values from -1.1953125 to 1.1953125
- step_size: float32 [8, 2048, 128], P('section', 'seq', 'head'), may hold values from 0.5 to 2
- log_decay: float32 [8, 2048, 128], P('section', 'seq', 'head'), may hold values from -3 to 0
- input_map: bfloat16 [8, 2048, 4, 256], P('section', 'seq', 'head'), may hold values from -0.375 to 0.375
- output_map: bfloat16 [8, 2048, 4, 256], P('section', 'seq', 'head'), may hold values from -0.375 to 0.375
- segment: int32 [8, 2048], P('section', 'seq'), may hold values from 0 to 7, never falling along the last dimension, each value on 1 to 1024 neighbouring positions
- sent_grad: bfloat16 [8, 2048, 8192], P('section', ('seq', 'head')), may hold values from -3 to 3
Outputs:
- grad_features: bfloat16 [8, 2048, 128, 64], P('section', 'seq', 'head')
- grad_step: float32 [8, 2048, 128], P('section', 'seq', 'head')
- grad_decay: float32 [8, 2048, 128], P('section', 'seq', 'head')
- grad_input_map: float32 [8, 2048, 4, 256], P('section', 'seq', 'head')
- grad_output_map: float32 [8, 2048, 4, 256], P('section', 'seq', 'head')
Inputs may be any that keep to these rules, and one draw needn't show every extreme that they name: `segment`: along each section's row the document numbers never fall; a document holds at most 1024 tokens, and one holds exactly that many.
All inputs are finite; a program needn't handle non-finite values.
Results may differ from a plain program's by a relative error of at most 0.039.
Values may be sent and summed in bfloat16 or wider, within the bound.
A program may use at most 192 MiB of HBM per device.

v0:
```python
import jax
import jax.numpy as jnp
from jax import lax
from jax.sharding import PartitionSpec as P

highest = lax.Precision.HIGHEST


def from_behind(block, axis, distance):
    devices = range(lax.axis_size(axis))
    route = [((i - distance) % len(devices), i) for i in devices]
    return lax.ppermute(block, axis, route)


def passed_along(array, axis, by):
    length = lax.axis_size(axis)
    pairs = [(i, i + by) for i in range(length) if 0 <= i + by < length]
    return lax.ppermute(array, axis, pairs)


def carried_in(array, axis, join, neutral, backward):
    count = lax.axis_size(axis)
    place = lax.axis_index(axis)
    ahead = count - 1 - place if backward else place
    gathered = jax.tree.map(
        lambda a, kind: lax.all_gather(a.astype(kind), axis),
        array,
        jax.tree.map(lambda a: jnp.bfloat16 if a.dtype == jnp.float32 else a.dtype, array),
    )
    state = jax.tree.map(lambda a, e: jnp.zeros_like(a) + jnp.asarray(e, a.dtype), array, neutral)

    def one(turn, state):
        source = count - 1 - turn if backward else turn
        return join(
            state,
            jax.tree.map(
                lambda a, own: lax.dynamic_index_in_dim(a, source, 0, False).astype(own.dtype),
                gathered,
                array,
            ),
        )

    return lax.fori_loop(0, ahead, one, state)


def layout(features, log_decay, segments, previous):
    length, heads, width = features.shape
    feat32 = features.astype(jnp.float32)
    cumulative = jnp.cumsum(log_decay, axis=0)
    carried = (segments == previous).astype(jnp.float32)
    token_positions = jnp.arange(length, dtype=jnp.int32)
    same_doc = (segments[:, None] == segments[None, :]) & (
        token_positions[:, None] >= token_positions[None, :]
    )
    along = cumulative.T
    log_gaps = along[:, :, None] - along[:, None, :]
    forward_mask = jnp.where(same_doc[None], jnp.exp(jnp.where(same_doc[None], log_gaps, 0.0)), 0.0)
    head_weight = carried[:, None] * jnp.exp(cumulative)
    tail_mask = (segments == segments[-1]).astype(jnp.float32)
    tail_weight = tail_mask[:, None] * jnp.exp(cumulative[-1][None, :] - cumulative)
    decay_total = carried[-1] * jnp.exp(cumulative[-1])
    return (feat32, forward_mask, head_weight, tail_weight, decay_total)


def by_group(array, groups):
    length, heads, width = array.shape
    return array.reshape(length, groups, heads // groups, width)


def state_summary(parts, step_size, in32, groups):
    feat32, forward_mask, head_weight, tail_weight, decay_total = parts
    length, heads, width = feat32.shape
    end_weight = forward_mask[:, -1, :].T * step_size
    weighted = by_group(end_weight[:, :, None] * feat32, groups)
    summary = jnp.einsum("tgn,tgrp->grnp", in32, weighted, precision=highest)
    return summary.reshape(heads, in32.shape[2], width)


def grad_summary(parts, grad32, out32, groups):
    feat32, forward_mask, head_weight, tail_weight, decay_total = parts
    length, heads, width = feat32.shape
    weighted = by_group(head_weight[:, :, None] * grad32, groups)
    summary = jnp.einsum("tgn,tgrp->grnp", out32, weighted, precision=highest)
    return summary.reshape(heads, out32.shape[2], width)


def low_product(form, left, right):
    return jnp.einsum(form, left, right, preferred_element_type=jnp.float32)


def finish(
    parts,
    feats,
    grad_low,
    grad32,
    step_size,
    in_low,
    out_low,
    in32,
    out32,
    state_in,
    grad_in,
    groups,
):
    feat32, forward_mask, head_weight, tail_weight, decay_total = parts
    length, heads, width = feat32.shape
    depth = in_low.shape[2]
    repeat = heads // groups
    state_four = state_in.reshape(groups, repeat, depth, width)
    grad_four = grad_in.reshape(groups, repeat, depth, width)
    backward_mask = jnp.swapaxes(forward_mask, 1, 2)
    cross = jnp.repeat(low_product("tgn,sgn->gts", in_low, out_low), repeat, axis=0)
    pairs = low_product("thp,shp->hts", grad_low, feats)
    lifted = low_product("tgn,grnp->tgrp", in_low, grad_four).reshape(length, heads, width)
    value = (
        jnp.einsum("htr,rhp->thp", backward_mask * cross, grad32, precision=highest)
        + tail_weight[:, :, None] * lifted
    )
    grad_features = (step_size[:, :, None] * value).astype(jnp.bfloat16)
    grad_step = jnp.sum(feat32 * value, axis=2)
    inner = step_size.T[:, :, None] * backward_mask * jnp.swapaxes(pairs, 1, 2)
    inner_group = inner.reshape(groups, repeat, length, length).sum(axis=1)
    into_first = jnp.einsum("gts,sgn->tgn", inner_group, out32, precision=highest)
    scaled_feats = by_group((step_size * tail_weight)[:, :, None] * feat32, groups)
    into_second = jnp.einsum(
        "tgrp,grnp->tgn", scaled_feats, grad_four.astype(jnp.float32), precision=highest
    )
    grad_in_map = into_first + into_second
    weighted = forward_mask * pairs * step_size.T[:, None, :]
    weighted_group = weighted.reshape(groups, repeat, length, length).sum(axis=1)
    out_first = jnp.einsum("gts,sgn->tgn", weighted_group, in32, precision=highest)
    scaled_grads = by_group(head_weight[:, :, None] * grad32, groups)
    out_second = jnp.einsum(
        "tgrp,grnp->tgn", scaled_grads, state_four.astype(jnp.float32), precision=highest
    )
    grad_out_map = out_first + out_second
    kernel = jnp.swapaxes(cross, 1, 2) * pairs * step_size.T[:, None, :]
    chained = jnp.einsum("htr,hrs->hts", backward_mask, kernel, precision=highest)
    first = jnp.sum(chained * forward_mask, axis=2).T
    seen = low_product("tgn,grnp->tgrp", out_low, state_four).reshape(length, heads, width)
    second = head_weight * jnp.einsum(
        "htr,rh->th", backward_mask, jnp.sum(seen * grad32, axis=2), precision=highest
    )
    third = tail_weight * jnp.einsum(
        "hts,sh->th", forward_mask, step_size * jnp.sum(lifted * feat32, axis=2), precision=highest
    )
    fourth = (
        tail_weight
        * head_weight
        * jnp.sum(grad_in.astype(jnp.float32) * state_in.astype(jnp.float32), axis=(1, 2))[None, :]
    )
    grad_decay = first + second + third + fourth - step_size * grad_step
    return (grad_features, grad_step, grad_decay, grad_in_map, grad_out_map)


def combine(earlier, later):
    decay_early = earlier[0].astype(jnp.float32)
    decay_late = later[0].astype(jnp.float32)
    state_early = earlier[1].astype(jnp.float32)
    state_late = later[1].astype(jnp.float32)
    joined = state_late + decay_late[:, None, None] * state_early
    return ((decay_early * decay_late).astype(jnp.bfloat16), joined.astype(jnp.bfloat16))


def per_device(features, step_size, log_decay, input_map, output_map, segment, sent_grad):
    moved = from_behind(sent_grad, "section", -1)
    received = lax.all_to_all(moved, "head", split_axis=2, concat_axis=1, tiled=True)
    feats = features[0]
    length, heads, width = feats.shape
    groups = input_map.shape[2]
    segments = segment[0]
    previous = passed_along(segments[-1:], "seq", 1)[0]
    steps_local = step_size[0]
    parts = layout(feats, log_decay[0], segments, previous)
    in_low = input_map[0]
    out_low = output_map[0]
    in32 = in_low.astype(jnp.float32)
    out32 = out_low.astype(jnp.float32)
    grad_low = received[0].reshape(length, heads, width)
    grad32 = grad_low.astype(jnp.float32)
    forward_pair = (
        parts[4].astype(jnp.bfloat16),
        state_summary(parts, steps_local, in32, groups).astype(jnp.bfloat16),
    )
    backward_pair = (
        parts[4].astype(jnp.bfloat16),
        grad_summary(parts, grad32, out32, groups).astype(jnp.bfloat16),
    )
    identity = (jnp.ones_like(forward_pair[0]), jnp.zeros_like(forward_pair[1]))
    state_in = carried_in(forward_pair, "seq", combine, identity, False)[1]
    grad_in = carried_in(backward_pair, "seq", combine, identity, True)[1]
    outs = finish(
        parts,
        feats,
        grad_low,
        grad32,
        steps_local,
        in_low,
        out_low,
        in32,
        out32,
        state_in,
        grad_in,
        groups,
    )
    return (outs[0][None], outs[1][None], outs[2][None], outs[3][None], outs[4][None])


def solution(mesh):
    placed = (
        P("section", "seq", "head", None),
        P("section", "seq", "head"),
        P("section", "seq", "head"),
        P("section", "seq", "head", None),
        P("section", "seq", "head", None),
        P("section", "seq"),
        P("section", ("seq", "head"), None),
    )
    return jax.shard_map(
        per_device,
        mesh=mesh,
        in_specs=placed,
        out_specs=(
            P("section", "seq", "head", None),
            P("section", "seq", "head"),
            P("section", "seq", "head"),
            P("section", "seq", "head", None),
            P("section", "seq", "head", None),
        ),
        check_vma=False,
    )
```

profile of v0, /device:TPU:31, one launch (start us, length us, event | category | flops | bytes accessed | tf_op | source)
XLA Modules:
  0.0 971.0 jit_solution(1197552264906262011)
XLA Ops:
  7.2 5.7 collective-permute-start
  24.2 10.8 %collective-permute-done = bf16[1,64,8192]{2,1,0:T(8,128)(2,1)S(1)} collective-permute-done((bf16[1,64,8192]{2,1,0:T(8,128)(2,1)}, bf16[1,64,8192]{2,1,0:T(8,128)(2,1)S(1)}, u32[]{:S(2)}, u32[]{:S(2)}) %collective-permute-start) | collective-permute-done | bytes 1048608 | tf_op jit(solution)/shard_map/ppermute | solution.py:12
  35.0 6.8 copy.283
  42.3 45.2 %reduce.8 = bf16[8192,64]{1,0:T(8,128)(2,1)S(1)} reduce(bf16[8192,1,64]{2,1,0:T(2,128)(2,1)} %bitcast.204, bf16[]{:T(256)} %broadcast.98), dimensions={1}, to_apply=%bitcast.163.reduce_sub_computation | reduce | bytes 2097154
  89.2 5.9 all_to_all.15
  129.8 15.3 %all-gather = bf16[16,1,64]{2,1,0:T(2,128)(2,1)S(1)} all-gather(bf16[1,1,64]{2,1,0:T(2,128)(2,1)S(1)} %copy-done.35), channel_id=1, replica_groups=mesh['section'=8,'seq'=16,'head'=2] {'seq'}, dimensions={0}, use_global_device_ids=true | all-gather | bytes 2176 | tf_op jit(solution)/shard_map/all_gather | solution.py:26
  145.6 169.2 %all-gather.4.cloned.1.call-done = bf16[16,64,256,64]{2,3,1,0:T(8,128)(2,1)} async-done(((bf16[1,64,256,64]{2,3,1,0:T(8,128)(2,1)}), bf16[16,64,256,64]{2,3,1,0:T(8,128)(2,1)}) %all-gather.4.cloned.1.call-update) | async-done | bytes 33554448 | tf_op jit(solution)/shard_map/all_gather | solution.py:26
  319.1 5.0 fusion.6
  327.6 5.6 copy.315
  333.3 4.9 copy.307
  347.8 11.5 %multiply_reduce_fusion.2 = f32[64,128]{1,0:T(8,128)S(1)} fusion(f32[64,128,128]{2,1,0:T(8,128)S(1)} %get-tuple-element.247, f32[64,128]{1,0:T(8,128)S(1)} %copy.278, pred[128,128]{0,1:T(8,128)(4,1)S(1)} %copy-done.25), kind=kOutput, calls=%fused_computation.17 | convolution fusion | flops 1618993152 | bytes 4276224 | tf_op jit(solution)/shard_map/htr,hrs->hts/dot_general | solution.py:138
  367.5 4.5 fusion.23
  379.6 356.8 %all-gather.6.cloned.1.call-done = bf16[16,64,256,64]{2,3,1,0:T(8,128)(2,1)} async-done(((bf16[1,64,256,64]{2,3,1,0:T(8,128)(2,1)}), bf16[16,64,256,64]{2,3,1,0:T(8,128)(2,1)}) %all-gather.6.cloned.1.call-update) | async-done | bytes 33554448 | tf_op jit(solution)/shard_map/all_gather | solution.py:26
  739.5 204.1 %while.27 = (s32[]{:T(128)}, bf16[64,256,64]{2,1,0:T(8,128)(2,1)}, s32[]{:T(128)}, bf16[16,64,256,64]{2,3,1,0:T(8,128)(2,1)}, bf16[16,64]{1,0:T(8,128)(2,1)}, /*index=5*/s32[]{:T(128)}, s32[]{:T(128)}, s32[]{:T(128)}) while((s32[]{:T(128)}, bf16[64,256,64]{2,1,0:T(8,128)(2,1)}, s32[]{:T(128)}, bf16[16,64,256,64]{2,3,1,0:T(8,128)(2,1)}, ...), condition=%wide.region_6.7_spmd, body=%wide.region_5.6_spmd.sunk | while | flops 5242949 | bytes 14680839 | solution.py:43
  745.1 8.0 fusion.65
  758.7 8.0 fusion.65
  772.3 8.0 fusion.65
  785.9 8.0 fusion.65
  799.5 8.0 fusion.65
  813.1 8.0 fusion.65
  826.7 8.0 fusion.65
  840.3 8.0 fusion.65
  853.9 8.0 fusion.65
  867.5 8.0 fusion.65
  881.1 8.0 fusion.65
  894.7 8.0 fusion.65
  908.3 8.0 fusion.65
  921.9 8.0 fusion.65
  935.5 8.0 fusion.65
  943.7 5.5 multiply_reduce_fusion
  949.1 4.4 convolution_bitcast_fusion
  956.3 6.7 fusion.3
  (179 shorter events, 172.8 us)
Async XLA Ops:
  7.2 105.2 %copy-start = (bf16[1,128,2,256]{3,2,1,0:T(2,128)(2,1)S(1)}, bf16[1,128,2,256]{3,2,1,0:T(2,128)(2,1)}, u32[]{:S(2)}) copy-start(bf16[1,128,2,256]{3,2,1,0:T(2,128)(2,1)} %param.15) | copy-start | bytes 393220
  7.2 307.6 %all-gather.4.cloned.1.call-start = ((), (), s32[]{:S(2)}) async-start(), calls=%async_computation.1 | async-start | bytes 35651584 | tf_op jit(solution)/shard_map/all_gather | solution.py:26
  7.2 27.8 %collective-permute-start = (bf16[1,64,8192]{2,1,0:T(8,128)(2,1)}, bf16[1,64,8192]{2,1,0:T(8,128)(2,1)S(1)}, u32[]{:S(2)}, u32[]{:S(2)}) collective-permute-start(bf16[1,64,8192]{2,1,0:T(8,128)(2,1)} %param.17), channel_id=1, source_target_pairs={{32,0},{64,32},{96,64},{128,96},{160,128},{192,160},{224,192},{0,2... | collective-permute-start | bytes 3145736 | tf_op jit(solution)/shard_map/ppermute | solution.py:12
  14.1 4.7 collective-permute-start.1
  20.7 21.1 %copy-start.27 = (f32[128]{0:T(128)}, f32[128]{0:T(128)S(1)}, u32[]{:S(2)}) copy-start(f32[128]{0:T(128)S(1)} %get-tuple-element.243) | copy-start | bytes 1540
  20.8 21.1 %copy-start.30 = (f32[128]{0:T(128)}, f32[128]{0:T(128)S(1)}, u32[]{:S(2)}) copy-start(f32[128]{0:T(128)S(1)} %get-tuple-element.244) | copy-start | bytes 1540
  112.4 7.9 copy-start.6
  112.4 4.0 copy-start.34
  112.4 4.1 copy-start.13
  115.6 620.8 %all-gather.6.cloned.1.call-start = ((), (), s32[]{:S(2)}) async-start(), calls=%async_computation.2 | async-start | bytes 35651584 | tf_op jit(solution)/shard_map/all_gather | solution.py:26
  116.6 3.8 copy-start.24
  116.8 3.6 copy-start.15
  125.3 4.4 copy-start.35
  318.1 6.1 copy-start.17
  318.1 6.1 copy-start.20
  327.5 5.7 copy-start.28
  327.5 5.6 copy-start.32
  333.2 5.1 copy-start.10
  338.3 6.6 copy-start.16
  363.4 4.1 copy-start.2
  363.5 4.1 copy-start.23
  367.5 5.7 copy-start.8
  367.5 5.7 copy-start.12
  376.8 362.7 %copy-start.22 = (f32[128,64]{0,1:T(8,128)}, f32[128,64]{0,1:T(8,128)S(1)}, u32[]{:S(2)}) copy-start(f32[128,64]{0,1:T(8,128)S(1)} %get-tuple-element.230) | copy-start | bytes 98308
  943.6 5.5 copy-start.1
  943.6 5.5 copy-start.7
  949.1 4.4 copy-start.11
  955.1 8.0 copy-start.18
  955.1 8.0 copy-start.21
  955.1 8.0 copy-start.29
  955.1 8.0 copy-start.31
  955.2 8.0 copy-start.33
  (8 other events, 20.4 us)
Sparse Core Ops, SparseCore 0:
  115.7 199.0 all-gather.3
  327.7 408.7 all-gather.5
where the time goes:
time: 978 us; the launch traced here: 971 us
  waiting for transfers between devices  539 us (55%)
  other arithmetic  203 us (21%)
  local copies, waits for them, and re-layouts  138 us (14%)
  matrix products  47 us (5%)
  blocking collectives  21.2 us (2%)
  between operations  14.8 us (2%)
    all_gather x2, waiting for transfers between devices, carried_in(): lax.all_gather(a.astype(kind), axis)  526 us
    convert_element_type x15, other arithmetic, combine(): joined.astype(jnp.bfloat16)  120 us
    dynamic_slice x30, local copies, waits for them, and re-layouts, one(): lax.dynamic_index_in_dim(a, source, 0, False).astype(own.dtype)  74.1 us
    unnamed x3, other arithmetic  47.8 us
  transfers between devices with their start and end apart: 4, of which 4 were waited for; matrix products, arithmetic and copies ran while one was open for 7% of the time, Pallas kernels for 0%

commit v1 on v0

v1 whole, which is shorter than its diff:
```python
import jax
import jax.numpy as jnp
from jax import lax
from jax.experimental import pallas as pl
from jax.experimental.pallas import tpu as pltpu
from jax.sharding import PartitionSpec as P

MESH = pl.DeviceIdType.MESH
F32 = jnp.float32
BF16 = jnp.bfloat16
HIGHEST = lax.Precision.HIGHEST

T = 128
W = 64
N = 256
ROW = 4
HEADS = 16
CHUNKS = 4
HC = HEADS // CHUNKS
CW = HC * W


def dot(a, b, precision=None):
    return lax.dot_general(
        a, b, (((1,), (0,)), ((), ())), precision=precision, preferred_element_type=F32
    )


def dot_nt(a, b, precision=None):
    return lax.dot_general(
        a, b, (((1,), (1,)), ((), ())), precision=precision, preferred_element_type=F32
    )


def dot_tn(a, b):
    return lax.dot_general(a, b, (((0,), (0,)), ((), ())), preferred_element_type=F32)


def place(s, y, x, c):
    return {
        "section": lax.rem(s + 8, 8),
        "seq": lax.rem(y + 4, 4) * 4 + lax.rem(x + 4, 4),
        "head": lax.rem(c, 2),
    }


def kernel(
    feat, step, dec, maps, seg, grad,
    gf_out, gs_out, gd_out, gim_out, gom_out,
    XT, XW, GRN, GRT, GHW, MAP, STEP, DEC, SEG, PREV,
    L, LT, HW, TW, STW, DB, CF, CB, CM, MASK, PRE,
    PF, PB, VI, WS, CK, RK, U, V, B4,
    EB, GB, ES, GS, GIM, GOM, PMS, PM, GF, GSS, GDS,
    ssem, rs_one, rs_feat, rs_grad, rs_f, rs_b,
):
    s = lax.axis_index("section")
    q = lax.axis_index("seq")
    c = lax.axis_index("head")
    y = q // 4
    x = lax.rem(q, 4)
    gl_mine = lax.rem(x, 2)
    co = x // 2
    R_SEG, R_STEP, R_DEC, R_MAP, R_PREV, R_GF, R_GS, R_GD, R_PM = range(9)

    barrier = pltpu.get_barrier_semaphore()
    for dx in range(4):
        for dc in range(2):
            if dx or dc:
                pl.semaphore_signal(barrier, inc=1, device_id=place(s, y, x + dx, c + dc), device_id_type=MESH)
            pl.semaphore_signal(barrier, inc=1, device_id=place(s + 1, y, x + dx, c + dc), device_id_type=MESH)
    for dy in (1, -1):
        pl.semaphore_signal(barrier, inc=1, device_id=place(s, y + dy, x, c), device_id_type=MESH)
    pl.semaphore_wait(barrier, 17)

    pending = []

    def send(src, dst, rsem, target, own=None):
        copy = pltpu.make_async_remote_copy(
            src_ref=src, dst_ref=dst, send_sem=ssem.at[len(pending)], recv_sem=rsem,
            device_id=target, device_id_type=MESH,
        )
        if own is None:
            copy.start()
            pending.append((None, copy))
        else:
            away = jnp.logical_not(own)

            @pl.when(own)
            def _():
                pltpu.make_async_copy(src, dst, rsem).start()

            @pl.when(away)
            def _():
                copy.start()

            pending.append((away, copy))

    def arrived(ref, sem):
        pltpu.make_async_copy(ref, ref, sem).wait()

    pltpu.make_async_copy(seg, SEG.at[x], rs_one.at[R_SEG]).start()
    for dx in range(1, 4):
        send(seg, SEG.at[x], rs_one.at[R_SEG], place(s, y, x + dx, c))
    workers = []
    for gl in range(2):
        for dc in range(2):
            xw = 2 * c + gl
            cw = lax.rem(c + dc, 2)
            workers.append((gl, xw, cw, (xw == x) if dc == 0 else None))
    for gl, xw, cw, own in workers:
        rows = pl.ds(pl.multiple_of(32 * gl + 16 * cw, 16), 16)
        send(step.at[rows], STEP.at[x], rs_one.at[R_STEP], place(s, y, xw, cw), own)
        send(dec.at[rows], DEC.at[x], rs_one.at[R_DEC], place(s, y, xw, cw), own)
    for gl, xw, cw, own in workers:
        send(maps.at[gl], MAP.at[x], rs_one.at[R_MAP], place(s, y, xw, cw), own)
    for k in range(CHUNKS):
        for gl, xw, cw, own in workers:
            rows = pl.ds(pl.multiple_of((32 * gl + 16 * cw + HC * k) * W, CW), CW)
            send(feat.at[rows], XT.at[k, x], rs_feat.at[k], place(s, y, xw, cw), own)
        for dx in range(4):
            for dc in range(2):
                xw = lax.rem(x + dx, 4)
                cw = lax.rem(c + dc, 2)
                cols = pl.ds(pl.multiple_of((32 * xw + 16 * cw + HC * k) * W, CW), CW)
                send(
                    grad.at[:, cols],
                    GRN.at[k, x, pl.ds(pl.multiple_of(64 * c, 64), 64), :],
                    rs_grad.at[k],
                    place(s - 1, y, xw, cw),
                )

    arrived(SEG, rs_one.at[R_SEG])
    send(SEG.at[3], PREV, rs_one.at[R_PREV], place(s, y + 1, x, c))
    arrived(STEP, rs_one.at[R_STEP])
    arrived(DEC, rs_one.at[R_DEC])
    row_id = lax.broadcasted_iota(jnp.int32, (T, T), 0)
    col_id = lax.broadcasted_iota(jnp.int32, (T, T), 1)
    upper = (row_id <= col_id).astype(F32)
    for b in range(ROW):
        total = dot(DEC[b], upper, HIGHEST)
        L[b] = total
        padded = jnp.concatenate([total, jnp.zeros((T - HEADS, T), F32)], axis=0)
        LT[b] = jnp.transpose(padded)
        seg_row = SEG[b][0:1, :]
        seg_col = jnp.transpose(jnp.broadcast_to(seg_row, (T, T)))
        same = (seg_col == seg_row).astype(F32)
        MASK[b] = jnp.where(row_id >= col_id, same, 0.0)
        PRE[b] = jnp.where(row_id < col_id, same, 0.0)
    arrived(PREV, rs_one.at[R_PREV])
    first = (y > 0).astype(F32)
    decays = []
    for b in range(ROW):
        total = L[b]
        seg_row = SEG[b][0:1, :]
        if b == 0:
            previous = PREV[0:1, T - 1 : T] * first
        else:
            previous = SEG[b - 1][0:1, T - 1 : T]
        last = total[:, T - 1 : T]
        seg_last = seg_row[:, T - 1 : T]
        carried = (seg_row == previous).astype(F32)
        tail = (seg_row == seg_last).astype(F32)
        HW[b] = carried * jnp.exp(total)
        tw = tail * jnp.exp(last - total)
        TW[b] = tw
        STW[b] = STEP[b] * tw
        d = jnp.broadcast_to((seg_last == previous).astype(F32) * jnp.exp(last), (HEADS, N))
        DB[b] = d
        decays.append(d)
    one = jnp.ones((HEADS, N), F32)
    run = one
    for b in range(ROW):
        CF[b] = run
        run = run * decays[b]
    CF[ROW] = run
    run = one
    for b in reversed(range(ROW)):
        CB[b] = run
        run = run * decays[b]
    arrived(MAP, rs_one.at[R_MAP])
    for b in range(ROW):
        CM[b] = dot_nt(MAP[b, 1], MAP[b, 0])
        WS[b] = jnp.zeros((T, T), F32)
        RK[b] = jnp.zeros((T, T), F32)
        GIM[b] = jnp.zeros((T, N), F32)
        GOM[b] = jnp.zeros((T, N), F32)

    def by_head(a):
        return a.reshape(HC, W, a.shape[-1])

    def scaled(a, w):
        return (by_head(a) * w[:, None, :]).reshape(a.shape)

    def heads_of(ref, b, k):
        return ref[b, HC * k : HC * (k + 1), :]

    def local_states(k):
        arrived(XT.at[k], rs_feat.at[k])
        total = jnp.zeros((CW, N), F32)
        PF[k, 0] = total
        for b in range(ROW):
            xw = scaled(XT[k, b].astype(F32), heads_of(STW, b, k)).astype(BF16)
            XW[k, b] = xw
            total = scaled(total, heads_of(DB, b, k)) + dot(xw, MAP[b, 0])
            PF[k, b + 1] = total

    def local_grads(k):
        arrived(GRN.at[k], rs_grad.at[k])
        total = jnp.zeros((CW, N), F32)
        PB[k, ROW] = total
        for b in reversed(range(ROW)):
            gt = jnp.transpose(GRN[k, b])
            GRT[k, b] = gt
            gh = scaled(gt.astype(F32), heads_of(HW, b, k)).astype(BF16)
            GHW[k, b] = gh
            total = scaled(total, heads_of(DB, b, k)) + dot(gh, MAP[b, 1])
            PB[k, b] = total

    def take_f(k):
        @pl.when(y > 0)
        def _():
            arrived(EB.at[k], rs_f.at[k])

        @pl.when(y == 0)
        def _():
            EB[k] = jnp.zeros((CW, N), BF16)

    def take_b(k):
        @pl.when(y < 3)
        def _():
            arrived(GB.at[k], rs_b.at[k])

        @pl.when(y == 3)
        def _():
            GB[k] = jnp.zeros((CW, N), BF16)

    fsend = {}
    bsend = {}

    def forward_f(k):
        entering = scaled(EB[k].astype(F32), heads_of(CF, ROW, k))
        ES[k] = (entering + PF[k, ROW]).astype(BF16)
        fsend[k].start()

    def forward_b(k):
        whole = heads_of(CF, ROW, k)
        entering = scaled(GB[k].astype(F32), whole)
        GS[k] = (entering + PB[k, 0]).astype(BF16)
        bsend[k].start()

    def prepare(k):
        n = len(pending)
        fsend[k] = pltpu.make_async_remote_copy(
            src_ref=ES.at[k], dst_ref=EB.at[k], send_sem=ssem.at[n], recv_sem=rs_f.at[k],
            device_id=place(s, y + 1, x, c), device_id_type=MESH,
        )
        pending.append((y < 3, fsend[k]))
        bsend[k] = pltpu.make_async_remote_copy(
            src_ref=GS.at[k], dst_ref=GB.at[k], send_sem=ssem.at[n + 1], recv_sem=rs_b.at[k],
            device_id=place(s, y - 1, x, c), device_id_type=MESH,
        )
        pending.append((y > 0, bsend[k]))

    def hop_f(k, at):
        @pl.when(y == at)
        def _():
            take_f(k)
            forward_f(k)

    def hop_b(k, at):
        @pl.when(y == at)
        def _():
            take_b(k)
            forward_b(k)

    def intra(k):
        def one_block(b, carry):
            xt = XT[k, b]
            zero = jnp.zeros((W, T), BF16)
            spread = jnp.concatenate(
                [
                    jnp.concatenate(
                        [xt[W * h : W * (h + 1)] if h == j else zero for j in range(HC)], axis=1
                    )
                    for h in range(HC)
                ],
                axis=0,
            )
            pairs = dot(GRN[k, b], spread)
            mask = MASK[b] > 0.0
            cross = CM[b]
            columns = LT[b]
            held = WS[b]
            sums = RK[b]
            lane = lax.broadcasted_iota(jnp.int32, (T, T), 1)
            cols = []
            for h in range(HC):
                head = HC * k + h
                gap = columns[:, head : head + 1] - L[b, head : head + 1, :]
                m = jnp.where(mask, jnp.exp(gap), 0.0)
                a = (m * cross).astype(BF16)
                VI[k, b, W * h : W * (h + 1), :] = dot(GRT[k, b, W * h : W * (h + 1), :], a)
                wh = m * pairs[:, T * h : T * (h + 1)] * STEP[b, head : head + 1, :]
                held = held + wh
                kk = wh * cross
                cols.append(jnp.sum(kk, axis=0, keepdims=True))
                sums = jnp.where(lane == head, jnp.sum(kk, axis=1, keepdims=True), sums)
            CK[b, HC * k : HC * (k + 1), :] = jnp.concatenate(cols, axis=0)
            WS[b] = held
            RK[b] = sums
            return carry

        lax.fori_loop(0, ROW, one_block, 0)

    def finish(k):
        def one_block(b, carry):
            e = EB[k].astype(F32)
            g = GB[k].astype(F32)
            eb = (PF[k, b] + scaled(e, heads_of(CF, b, k))).astype(BF16)
            gb = (PB[k, b + 1] + scaled(g, heads_of(CB, b, k))).astype(BF16)
            lift = dot_nt(gb, MAP[b, 0])
            seen = dot_nt(eb, MAP[b, 1])
            val = VI[k, b] + scaled(lift, heads_of(TW, b, k))
            GF[k, b] = scaled(val, heads_of(STEP, b, k)).astype(BF16)
            hs = slice(HC * k, HC * (k + 1))
            V[b, hs, :] = heads_of(STW, b, k) * jnp.sum(by_head(XT[k, b].astype(F32) * lift), axis=1)
            U[b, hs, :] = heads_of(HW, b, k) * jnp.sum(by_head(GRT[k, b].astype(F32) * seen), axis=1)
            both = jnp.sum(by_head(eb.astype(F32) * gb.astype(F32)), axis=1)
            B4[b, hs, :] = jnp.broadcast_to(jnp.sum(both, axis=1, keepdims=True), (HC, T))
            GIM[b] += dot_tn(XW[k, b], gb)
            GOM[b] += dot_tn(GHW[k, b], eb)
            return carry

        lax.fori_loop(0, ROW, one_block, 0)
        for dx in range(4):
            xo = lax.rem(x + dx, 4)
            rows = pl.ds(pl.multiple_of((32 * gl_mine + 16 * c + HC * k) * W, CW), CW)
            send(
                GF.at[k, xo], gf_out.at[rows], rs_one.at[R_GF],
                place(s, y, xo, co), (c == co) if dx == 0 else None,
            )

    for k in range(CHUNKS):
        prepare(k)
    for k in range(CHUNKS + 2):
        if k < CHUNKS:
            local_states(k)
            hop_f(k, 0)
            local_grads(k)
            hop_b(k, 3)
            intra(k)
        if 0 <= k - 1 < CHUNKS:
            hop_b(k - 1, 1)
            hop_f(k - 1, 2)
        if k < CHUNKS:
            hop_f(k, 1)
            hop_b(k, 2)
        if 0 <= k - 2:
            @pl.when(y == 0)
            def _():
                take_b(k - 2)

            @pl.when(y == 3)
            def _():
                take_f(k - 2)

            finish(k - 2)

    for b in range(ROW):
        w = WS[b].astype(BF16)
        PMS[b, 0] = (GIM[b] + dot_tn(w, MAP[b, 1])).astype(BF16)
        PMS[b, 1] = (GOM[b] + dot(w, MAP[b, 0])).astype(BF16)
    for dx in range(4):
        xo = lax.rem(x + dx, 4)
        own = (c == co) if dx == 0 else None
        send(PMS.at[xo], PM.at[gl_mine, c], rs_one.at[R_PM], place(s, y, xo, co), own)
    for b in range(ROW):
        row_sums = jnp.transpose(RK[b])[0:HEADS, :]
        ck = CK[b]
        v = V[b]
        GSS[b] = (ck + v) / STEP[b]
        chain = dot(row_sums - ck + U[b], MASK[b], HIGHEST) + dot(v, PRE[b], HIGHEST)
        GDS[b] = chain + HW[b] * TW[b] * B4[b]
    for dx in range(4):
        xo = lax.rem(x + dx, 4)
        own = (c == co) if dx == 0 else None
        rows = pl.ds(pl.multiple_of(32 * gl_mine + 16 * c, 16), 16)
        send(GSS.at[xo], gs_out.at[rows], rs_one.at[R_GS], place(s, y, xo, co), own)
        send(GDS.at[xo], gd_out.at[rows], rs_one.at[R_GD], place(s, y, xo, co), own)

    arrived(PM, rs_one.at[R_PM])
    for gl in range(2):
        gim_out[gl] = PM[gl, 0, 0].astype(F32) + PM[gl, 1, 0].astype(F32)
        gom_out[gl] = PM[gl, 0, 1].astype(F32) + PM[gl, 1, 1].astype(F32)
    arrived(gf_out, rs_one.at[R_GF])
    arrived(gs_out, rs_one.at[R_GS])
    arrived(gd_out, rs_one.at[R_GD])
    for cond, copy in pending:
        if cond is None:
            copy.wait_send()
        else:
            @pl.when(cond)
            def _():
                copy.wait_send()


def per_device(features, step_size, log_decay, input_map, output_map, segment, sent_grad):
    feat = jnp.transpose(features[0], (1, 2, 0)).reshape(64 * W, T)
    step = step_size[0].T
    dec = log_decay[0].T
    maps = jnp.transpose(jnp.stack([input_map[0], output_map[0]]), (2, 0, 1, 3))
    seg = jnp.broadcast_to(segment.astype(F32), (8, T))
    grad = sent_grad[0]
    any_ = pl.BlockSpec(memory_space=pl.ANY)
    vmem = pl.BlockSpec(memory_space=pltpu.VMEM)
    V_ = pltpu.VMEM
    scratch = [
        V_((CHUNKS, ROW, CW, T), BF16),
        V_((CHUNKS, ROW, CW, T), BF16),
        V_((CHUNKS, ROW, T, CW), BF16),
        V_((CHUNKS, ROW, CW, T), BF16),
        V_((CHUNKS, ROW, CW, T), BF16),
        V_((ROW, 2, T, N), BF16),
        V_((ROW, HEADS, T), F32),
        V_((ROW, HEADS, T), F32),
        V_((ROW, 8, T), F32),
        V_((8, T), F32),
        V_((ROW, HEADS, T), F32),
        V_((ROW, T, T), F32),
        V_((ROW, HEADS, T), F32),
        V_((ROW, HEADS, T), F32),
        V_((ROW, HEADS, T), F32),
        V_((ROW, HEADS, N), F32),
        V_((ROW + 1, HEADS, N), F32),
        V_((ROW, HEADS, N), F32),
        V_((ROW, T, T), F32),
        V_((ROW, T, T), F32),
        V_((ROW, T, T), F32),
        V_((CHUNKS, ROW + 1, CW, N), F32),
        V_((CHUNKS, ROW + 1, CW, N), F32),
        V_((CHUNKS, ROW, CW, T), F32),
        V_((ROW, T, T), F32),
        V_((ROW, HEADS, T), F32),
        V_((ROW, T, T), F32),
        V_((ROW, HEADS, T), F32),
        V_((ROW, HEADS, T), F32),
        V_((ROW, HEADS, T), F32),
        V_((CHUNKS, CW, N), BF16),
        V_((CHUNKS, CW, N), BF16),
        V_((CHUNKS, CW, N), BF16),
        V_((CHUNKS, CW, N), BF16),
        V_((ROW, T, N), F32),
        V_((ROW, T, N), F32),
        V_((ROW, 2, T, N), BF16),
        V_((2, 2, 2, T, N), BF16),
        V_((CHUNKS, ROW, CW, T), BF16),
        V_((ROW, HEADS, T), F32),
        V_((ROW, HEADS, T), F32),
        pltpu.SemaphoreType.DMA((112,)),
        pltpu.SemaphoreType.DMA((9,)),
        pltpu.SemaphoreType.DMA((CHUNKS,)),
        pltpu.SemaphoreType.DMA((CHUNKS,)),
        pltpu.SemaphoreType.DMA((CHUNKS,)),
        pltpu.SemaphoreType.DMA((CHUNKS,)),
    ]
    gf, gs, gd, gim, gom = pl.pallas_call(
        kernel,
        out_shape=(
            jax.ShapeDtypeStruct((64 * W, T), BF16),
            jax.ShapeDtypeStruct((64, T), F32),
            jax.ShapeDtypeStruct((64, T), F32),
            jax.ShapeDtypeStruct((2, T, N), F32),
            jax.ShapeDtypeStruct((2, T, N), F32),
        ),
        in_specs=[any_, vmem, vmem, vmem, vmem, any_],
        out_specs=(any_, vmem, vmem, vmem, vmem),
        scratch_shapes=scratch,
        compiler_params=pltpu.CompilerParams(
            collective_id=0, has_side_effects=True, vmem_limit_bytes=50 * 2**20
        ),
        name="ssd_backward",
    )(feat, step, dec, maps, seg, grad)
    return (
        jnp.transpose(gf.reshape(64, W, T), (2, 0, 1))[None],
        gs.T[None],
        gd.T[None],
        jnp.transpose(gim, (1, 0, 2))[None],
        jnp.transpose(gom, (1, 0, 2))[None],
    )


def solution(mesh):
    placed = (
        P("section", "seq", "head", None),
        P("section", "seq", "head"),
        P("section", "seq", "head"),
        P("section", "seq", "head", None),
        P("section", "seq", "head", None),
        P("section", "seq"),
        P("section", ("seq", "head"), None),
    )
    return jax.shard_map(
        per_device,
        mesh=mesh,
        in_specs=placed,
        out_specs=(
            P("section", "seq", "head", None),
            P("section", "seq", "head"),
            P("section", "seq", "head"),
            P("section", "seq", "head", None),
            P("section", "seq", "head", None),
        ),
        check_vma=False,
    )
```

time: 978 us -> 81 us (0.08)
  the two profiles are of different devices: /device:TPU:31 before, /device:TPU:1 now
where the time goes in v1:
time: 81 us; the launch traced here: 80.7 us
  Pallas kernels  70.6 us (87%)
  local copies, waits for them, and re-layouts  8.59 us (11%)
    pallas_call x1, Pallas kernels, per_device(): pl.pallas_call(kernel, out_shape=(jax.ShapeDtypeStruct((64 * W, T), BF16)...  70.6 us
    unnamed x15, local copies, waits for them, and re-layouts  8.59 us

profile of v1, /device:TPU:1, one launch (start us, length us, event | category | flops | bytes accessed | tf_op | source)
XLA Modules:
  0.0 80.7 jit_solution(13902106224898750558)
XLA Ops:
  0.6 0.0 copy-start
  0.6 0.7 convert_bitcast_fusion
  1.4 0.9 %copy.12 = bf16[1,128,2,256]{3,1,0,2:T(8,128)(2,1)S(1)} copy(bf16[1,128,2,256]{3,2,1,0:T(2,128)(2,1)} %param.10) | data formatting | bytes 262144 | tf_op args[3]
  2.3 0.9 %copy.13 = bf16[1,128,2,256]{3,1,0,2:T(8,128)(2,1)S(1)} copy(bf16[1,128,2,256]{3,2,1,0:T(2,128)(2,1)} %param.11) | data formatting | bytes 262144 | tf_op args[4]
  3.3 0.0 copy-done
  3.3 0.0 copy-start.1
  3.3 1.2 %copy-done.1 = bf16[1,64,8192]{2,1,0:T(8,128)(2,1)S(1)} copy-done((bf16[1,64,8192]{2,1,0:T(8,128)(2,1)S(1)}, bf16[1,64,8192]{2,1,0:T(8,128)(2,1)}, u32[]{:S(2)}) %copy-start.1) | copy-done | bytes 1048600
  4.5 0.0 copy-start.2
  4.5 0.8 copy-done.2
  5.3 0.0 copy-start.3
  5.3 0.8 copy-done.3
  6.0 70.6 %ssd_backward.1 = (bf16[4096,128]{1,0:T(8,128)(2,1)S(1)}, f32[64,128]{1,0:T(8,128)S(1)}, f32[64,128]{1,0:T(8,128)S(1)}, f32[2,128,256]{2,1,0:T(8,128)S(1)}, f32[2,128,256]{2,1,0:T(8,128)S(1)}) custom-call(bf16[4096,128]{1,0:T(8,128)(2,1)S(1)} %bitcast.33, f32[64,128]{1,0:T(8,128)S(1)} %bitcast.38, f32[64,128]{1,0:T(8,128)S(1)} %bitcast.39, ...), custom_call_target="tpu_custom_call" | custom-call | tf_op jit(solution)/shard_map/ssd_backward/pallas_call | solution.py:466
  76.6 0.9 %copy.14 = f32[1,128,2,256]{3,2,1,0:T(2,128)} copy(f32[1,128,2,256]{3,1,2,0:T(8,128)S(1)} %bitcast.37) | data formatting | bytes 524288
  77.5 0.9 %copy.15 = f32[1,128,2,256]{3,2,1,0:T(2,128)} copy(f32[1,128,2,256]{3,1,2,0:T(8,128)S(1)} %bitcast.36) | data formatting | bytes 524288
  78.5 1.0 %copy.19 = bf16[1,128,64,64]{1,3,2,0:T(8,128)(2,1)} copy(bf16[1,128,64,64]{1,3,2,0:T(8,128)(2,1)S(1)} %bitcast.35) | data formatting | bytes 2097152
  79.4 0.6 copy.20
  80.0 0.6 copy.21
  (2 shorter events, 0.0 us)
Async XLA Ops:
  0.6 2.6 %copy-start = (bf16[1,128,64,64]{1,3,2,0:T(8,128)(2,1)S(1)}, bf16[1,128,64,64]{1,3,2,0:T(8,128)(2,1)}, u32[]{:S(2)}) copy-start(bf16[1,128,64,64]{1,3,2,0:T(8,128)(2,1)} %param.7) | copy-start | bytes 3145732
  3.3 1.2 %copy-start.1 = (bf16[1,64,8192]{2,1,0:T(8,128)(2,1)S(1)}, bf16[1,64,8192]{2,1,0:T(8,128)(2,1)}, u32[]{:S(2)}) copy-start(bf16[1,64,8192]{2,1,0:T(8,128)(2,1)} %param.13) | copy-start | bytes 3145732
  4.5 0.8 copy-start.2
  5.3 0.8 copy-start.3

commit v2 on v1

v2 whole, which is shorter than its diff:
```python
import itertools

import jax
import jax.numpy as jnp
from jax import lax
from jax.experimental import pallas as pl
from jax.experimental.pallas import tpu as pltpu
from jax.sharding import PartitionSpec as P

MESH = pl.DeviceIdType.MESH
F32 = jnp.float32
BF16 = jnp.bfloat16
HIGHEST = lax.Precision.HIGHEST

T = 128
W = 64
N = 256
ROW = 4
HEADS = 16
CHUNKS = 8
HC = HEADS // CHUNKS
WINDOW = 3
LAG = 2
CW = HC * W
FBASE = 40 + 8 * CHUNKS


def dot(a, b, precision=None):
    return lax.dot_general(
        a, b, (((1,), (0,)), ((), ())), precision=precision, preferred_element_type=F32
    )


def dot_nt(a, b, precision=None):
    return lax.dot_general(
        a, b, (((1,), (1,)), ((), ())), precision=precision, preferred_element_type=F32
    )


def dot_tn(a, b):
    return lax.dot_general(a, b, (((0,), (0,)), ((), ())), preferred_element_type=F32)


def place(s, y, x, c):
    return {
        "section": lax.rem(s + 8, 8),
        "seq": lax.rem(y + 4, 4) * 4 + lax.rem(x + 4, 4),
        "head": lax.rem(c, 2),
    }


def kernel(
    feat, step, dec, map_in, map_out, seg, grad,
    gf_out, gs_out, gd_out, PM,
    XT, XW, GRN, GRT, GHW, MAP, STEP, DEC, SEG, PREV,
    L, LT, HW, TW, STW, DB, CF, CB, CM, MASK, PRE,
    PF, PB, VI, WS, CK, RK, U, V, B4,
    RF, RB, ES, GS, EA, GA, EB, COF, COB, RDEC, ROWD,
    GIM, GOM, PMS, GF, GSS, GDS, SEGI, SEGF, RAW, MAPS,
    ssem, rs_one, ss_grad, rs_feat, rs_grad, rs_f, rs_b, ready,
):
    s = lax.axis_index("section")
    q = lax.axis_index("seq")
    c = lax.axis_index("head")
    y = q // 4
    x = lax.rem(q, 4)
    first_head = 16 * x
    R_SEG, R_STEP, R_DEC, R_MAP, R_PREV, R_GF, R_GS, R_GD, R_PM, R_RD, R_A, R_B, R_C = range(13)

    barrier = pltpu.get_barrier_semaphore()
    load_seg = pltpu.make_async_copy(seg, SEGI, rs_one.at[R_A])
    load_in = pltpu.make_async_copy(map_in, RAW.at[0], rs_one.at[R_B])
    load_out = pltpu.make_async_copy(map_out, RAW.at[1], rs_one.at[R_C])
    load_seg.start()
    load_in.start()
    load_out.start()

    def greet(target):
        pl.semaphore_signal(barrier, inc=1, device_id=target, device_id_type=MESH)

    for dx in range(1, 4):
        greet(place(s, y, x + dx, 0))

    @pl.when(c == 1)
    def _():
        greet(place(s, y, x, 0))

    for dx in range(4):
        greet(place(s + 1, y, x + dx, 1))
    for dy in range(1, 4):
        greet(place(s, y + dy, x, 1))

    load_seg.wait()
    SEGF[...] = jnp.broadcast_to(SEGI[...].astype(F32), (8, T))
    load_in.wait()
    load_out.wait()
    for g in range(2):
        MAPS[g, 0] = RAW[0, :, g, :]
        MAPS[g, 1] = RAW[1, :, g, :]

    @pl.when(c == 0)
    def _():
        pl.semaphore_wait(barrier, 7)
        pl.semaphore_signal(ready, inc=1, device_id=place(s, y, x, 1), device_id_type=MESH)

    @pl.when(c == 1)
    def _():
        pl.semaphore_wait(ready, 1)

    pending = []
    count = itertools.count()

    def send(src, dst, rsem, target):
        copy = pltpu.make_async_remote_copy(
            src_ref=src, dst_ref=dst, send_sem=ssem.at[next(count)], recv_sem=rsem,
            device_id=target, device_id_type=MESH,
        )
        copy.start()
        pending.append(copy)

    def arrived(ref, sem):
        pltpu.make_async_copy(ref, ref, sem).wait()

    pltpu.make_async_copy(SEGF, SEG.at[x], rs_one.at[R_SEG]).start()
    for dx in range(1, 4):
        send(SEGF, SEG.at[x], rs_one.at[R_SEG], place(s, y, x + dx, c))
    workers = [lax.rem(x + dx, 4) for dx in range(4)]

    def to_worker(src, dst, rsem, dx):
        if dx == 0:
            pltpu.make_async_copy(src, dst, rsem).start()
        else:
            send(src, dst, rsem, place(s, y, workers[dx], c))

    for dx in range(4):
        rows = pl.ds(pl.multiple_of(16 * workers[dx], 16), 16)
        to_worker(step.at[rows], STEP.at[x], rs_one.at[R_STEP], dx)
        to_worker(dec.at[rows], DEC.at[x], rs_one.at[R_DEC], dx)
    for dx in range(4):
        to_worker(MAPS.at[workers[dx] // 2], MAP.at[x], rs_one.at[R_MAP], dx)
    feat_sends = {}

    def issue_feat(k):
        before = len(pending)
        for dx in range(4):
            rows = pl.ds(pl.multiple_of((16 * workers[dx] + HC * k) * W, CW), CW)
            to_worker(feat.at[rows], XT.at[k, x], rs_feat.at[k], dx)
        feat_sends[k] = pending[before:]
        del pending[before:]

    def issue_grad(k):
        for dx in range(4):
            for dc in range(2):
                xw = lax.rem(x + dx, 4)
                cw = lax.rem(c + dc, 2)
                cols = pl.ds(pl.multiple_of((64 * cw + 16 * xw + HC * k) * W, CW), CW)
                pltpu.make_async_remote_copy(
                    src_ref=grad.at[:, cols],
                    dst_ref=GRN.at[k, x, pl.ds(pl.multiple_of(64 * c, 64), 64), :],
                    send_sem=ss_grad.at[k],
                    recv_sem=rs_grad.at[k],
                    device_id=place(s - 1, y, xw, cw),
                    device_id_type=MESH,
                ).start()

    def gone(k):
        for copy in feat_sends[k]:
            copy.wait_send()
        arrived(grad.at[:, pl.ds(0, 8 * CW)], ss_grad.at[k])

    for k in range(WINDOW):
        issue_feat(k)

    @pl.when(c == 1)
    def _():
        pl.semaphore_wait(barrier, 14)
        pl.semaphore_signal(ready, inc=1, device_id=place(s, y, x, 0), device_id_type=MESH)

    @pl.when(c == 0)
    def _():
        pl.semaphore_wait(ready, 1)

    for k in range(WINDOW):
        issue_grad(k)

    arrived(SEG, rs_one.at[R_SEG])
    send(SEG.at[3], PREV, rs_one.at[R_PREV], place(s, y + 1, x, c))
    arrived(STEP, rs_one.at[R_STEP])
    arrived(DEC, rs_one.at[R_DEC])
    row_id = lax.broadcasted_iota(jnp.int32, (T, T), 0)
    col_id = lax.broadcasted_iota(jnp.int32, (T, T), 1)
    upper = (row_id <= col_id).astype(F32)
    for b in range(ROW):
        total = dot(DEC[b], upper, HIGHEST)
        L[b] = total
        padded = jnp.concatenate([total, jnp.zeros((T - HEADS, T), F32)], axis=0)
        LT[b] = jnp.transpose(padded)
        seg_row = SEG[b][0:1, :]
        seg_col = jnp.transpose(jnp.broadcast_to(seg_row, (T, T)))
        same = (seg_col == seg_row).astype(F32)
        MASK[b] = jnp.where(row_id >= col_id, same, 0.0)
        PRE[b] = jnp.where(row_id < col_id, same, 0.0)
    arrived(PREV, rs_one.at[R_PREV])
    first = (y > 0).astype(F32)
    decays = []
    for b in range(ROW):
        total = L[b]
        seg_row = SEG[b][0:1, :]
        if b == 0:
            previous = PREV[0:1, T - 1 : T] * first
        else:
            previous = SEG[b - 1][0:1, T - 1 : T]
        last = total[:, T - 1 : T]
        seg_last = seg_row[:, T - 1 : T]
        carried = (seg_row == previous).astype(F32)
        tail = (seg_row == seg_last).astype(F32)
        HW[b] = carried * jnp.exp(total)
        tw = tail * jnp.exp(last - total)
        TW[b] = tw
        STW[b] = STEP[b] * tw
        d = jnp.broadcast_to((seg_last == previous).astype(F32) * jnp.exp(last), (HEADS, N))
        DB[b] = d
        decays.append(d)
    one = jnp.ones((HEADS, N), F32)
    run = one
    for b in range(ROW):
        CF[b] = run
        run = run * decays[b]
    CF[ROW] = run
    run = one
    for b in reversed(range(ROW)):
        CB[b] = run
        run = run * decays[b]
    ROWD[...] = CF[ROW][:, 0:T]
    pltpu.make_async_copy(ROWD, RDEC.at[y], rs_one.at[R_RD]).start()
    for dy in range(1, 4):
        send(ROWD, RDEC.at[y], rs_one.at[R_RD], place(s, y + dy, x, c))
    arrived(MAP, rs_one.at[R_MAP])
    for b in range(ROW):
        CM[b] = dot_nt(MAP[b, 1], MAP[b, 0])
        WS[b] = jnp.zeros((T, T), F32)
        RK[b] = jnp.zeros((T, T), F32)
        GIM[b] = jnp.zeros((T, N), F32)
        GOM[b] = jnp.zeros((T, N), F32)

    def by_head(a):
        return a.reshape(HC, W, a.shape[-1])

    def scaled(a, w):
        return (by_head(a) * w[:, None, :]).reshape(a.shape)

    def heads_of(ref, b, k):
        return ref[b, HC * k : HC * (k + 1), :]

    def copy_f(k, to):
        return pltpu.make_async_remote_copy(
            src_ref=ES.at[k], dst_ref=RF.at[k, y], send_sem=ssem.at[FBASE + 6 * k + to - 1],
            recv_sem=rs_f.at[k, y], device_id=place(s, to, x, c), device_id_type=MESH,
        )

    def copy_b(k, to):
        return pltpu.make_async_remote_copy(
            src_ref=GS.at[k], dst_ref=RB.at[k, y - 1], send_sem=ssem.at[FBASE + 6 * k + 3 + to],
            recv_sem=rs_b.at[k, y - 1], device_id=place(s, to, x, c), device_id_type=MESH,
        )

    def local_states(k):
        arrived(XT.at[k], rs_feat.at[k])
        total = jnp.zeros((CW, N), F32)
        PF[k, 0] = total
        for b in range(ROW):
            xw = scaled(XT[k, b].astype(F32), heads_of(STW, b, k)).astype(BF16)
            XW[k, b] = xw
            total = scaled(total, heads_of(DB, b, k)) + dot(xw, MAP[b, 0])
            PF[k, b + 1] = total
        ES[k] = total.astype(BF16)
        for to in range(1, 4):
            @pl.when(y < to)
            def _(to=to):
                copy_f(k, to).start()

    def local_grads(k):
        arrived(GRN.at[k], rs_grad.at[k])
        total = jnp.zeros((CW, N), F32)
        PB[k, ROW] = total
        for b in reversed(range(ROW)):
            gt = jnp.transpose(GRN[k, b])
            GRT[k, b] = gt
            gh = scaled(gt.astype(F32), heads_of(HW, b, k)).astype(BF16)
            GHW[k, b] = gh
            total = scaled(total, heads_of(DB, b, k)) + dot(gh, MAP[b, 1])
            PB[k, b] = total
        GS[k] = total.astype(BF16)
        for to in range(3):
            @pl.when(y > to)
            def _(to=to):
                copy_b(k, to).start()

    def enter_f(k):
        EA[...] = jnp.zeros((CW, N), F32)
        for src in range(3):
            @pl.when(y > src)
            def _(src=src):
                arrived(RF.at[k, src], rs_f.at[k, src])
                coef = COF[src, HC * k : HC * (k + 1), :]
                EA[...] += scaled(RF[k, src].astype(F32), coef)

    def enter_b(k):
        GA[...] = jnp.zeros((CW, N), F32)
        for src in range(1, 4):
            @pl.when(y < src)
            def _(src=src):
                arrived(RB.at[k, src - 1], rs_b.at[k, src - 1])
                coef = COB[src - 1, HC * k : HC * (k + 1), :]
                GA[...] += scaled(RB[k, src - 1].astype(F32), coef)

    def intra(k):
        def one_block(b, carry):
            xt = XT[k, b]
            zero = jnp.zeros((W, T), BF16)
            spread = jnp.concatenate(
                [
                    jnp.concatenate(
                        [xt[W * h : W * (h + 1)] if h == j else zero for j in range(HC)], axis=1
                    )
                    for h in range(HC)
                ],
                axis=0,
            )
            pairs = dot(GRN[k, b], spread)
            mask = MASK[b] > 0.0
            cross = CM[b]
            columns = LT[b]
            held = WS[b]
            sums = RK[b]
            lane = lax.broadcasted_iota(jnp.int32, (T, T), 1)
            cols = []
            for h in range(HC):
                head = HC * k + h
                gap = columns[:, head : head + 1] - L[b, head : head + 1, :]
                m = jnp.where(mask, jnp.exp(gap), 0.0)
                a = (m * cross).astype(BF16)
                VI[k, b, W * h : W * (h + 1), :] = dot(GRT[k, b, W * h : W * (h + 1), :], a)
                wh = m * pairs[:, T * h : T * (h + 1)] * STEP[b, head : head + 1, :]
                held = held + wh
                kk = wh * cross
                cols.append(jnp.sum(kk, axis=0, keepdims=True))
                sums = jnp.where(lane == head, jnp.sum(kk, axis=1, keepdims=True), sums)
            CK[b, HC * k : HC * (k + 1), :] = jnp.concatenate(cols, axis=0)
            WS[b] = held
            RK[b] = sums
            return carry

        lax.fori_loop(0, ROW, one_block, 0)

    def row_factors():
        arrived(RDEC, rs_one.at[R_RD])
        one = jnp.ones((HEADS, T), F32)
        for src in range(3):
            coef = one
            for r in range(src + 1, 3):
                coef = coef * jnp.where(y > r, RDEC[r], one)
            COF[src] = jnp.concatenate([coef, coef], axis=1)
            coef = one
            for r in range(1, src + 1):
                coef = coef * jnp.where(y < r, RDEC[r], one)
            COB[src] = jnp.concatenate([coef, coef], axis=1)

    def finish_f(k):
        enter_f(k)

        def one_block(b, carry):
            eb = (PF[k, b] + scaled(EA[...], heads_of(CF, b, k))).astype(BF16)
            EB[k, b] = eb
            seen = dot_nt(eb, MAP[b, 1])
            hs = slice(HC * k, HC * (k + 1))
            U[b, hs, :] = heads_of(HW, b, k) * jnp.sum(by_head(GRT[k, b].astype(F32) * seen), axis=1)
            GOM[b] += dot_tn(GHW[k, b], eb)
            return carry

        lax.fori_loop(0, ROW, one_block, 0)

    def finish_b(k):
        enter_b(k)

        def one_block(b, carry):
            gb = (PB[k, b + 1] + scaled(GA[...], heads_of(CB, b, k))).astype(BF16)
            lift = dot_nt(gb, MAP[b, 0])
            val = VI[k, b] + scaled(lift, heads_of(TW, b, k))
            GF[k, b] = scaled(val, heads_of(STEP, b, k)).astype(BF16)
            hs = slice(HC * k, HC * (k + 1))
            V[b, hs, :] = heads_of(STW, b, k) * jnp.sum(by_head(XT[k, b].astype(F32) * lift), axis=1)
            both = jnp.sum(by_head(EB[k, b].astype(F32) * gb.astype(F32)), axis=1)
            B4[b, hs, :] = jnp.broadcast_to(jnp.sum(both, axis=1, keepdims=True), (HC, T))
            GIM[b] += dot_tn(XW[k, b], gb)
            return carry

        lax.fori_loop(0, ROW, one_block, 0)
        for dx in range(4):
            rows = pl.ds(pl.multiple_of((first_head + HC * k) * W, CW), CW)
            to_worker(GF.at[k, workers[dx]], gf_out.at[rows], rs_one.at[R_GF], dx)

    def send_map(m):
        for dx in range(4):
            to_worker(PMS.at[workers[dx], m], PM.at[x // 2, lax.rem(x, 2), m], rs_one.at[R_PM], dx)

    for k in range(CHUNKS):
        local_states(k)
        local_grads(k)
        gone(k)
        if k + WINDOW < CHUNKS:
            issue_feat(k + WINDOW)
            issue_grad(k + WINDOW)
        intra(k)
        if k == 0:
            row_factors()
        if k >= LAG:
            finish_f(k - LAG)
            finish_b(k - LAG)
    for k in range(CHUNKS - LAG, CHUNKS):
        finish_f(k)
        if k + 1 == CHUNKS:
            for b in range(ROW):
                PMS[b, 1] = (GOM[b] + dot(WS[b].astype(BF16), MAP[b, 0])).astype(BF16)
            send_map(1)
        finish_b(k)
    for b in range(ROW):
        PMS[b, 0] = (GIM[b] + dot_tn(WS[b].astype(BF16), MAP[b, 1])).astype(BF16)
    send_map(0)

    for b in range(ROW):
        row_sums = jnp.transpose(RK[b])[0:HEADS, :]
        ck = CK[b]
        v = V[b]
        GSS[b] = (ck + v) / STEP[b]
        chain = dot(row_sums - ck + U[b], MASK[b], HIGHEST) + dot(v, PRE[b], HIGHEST)
        GDS[b] = chain + HW[b] * TW[b] * B4[b]
    for dx in range(4):
        rows = pl.ds(pl.multiple_of(first_head, 16), 16)
        to_worker(GSS.at[workers[dx]], gs_out.at[rows], rs_one.at[R_GS], dx)
        to_worker(GDS.at[workers[dx]], gd_out.at[rows], rs_one.at[R_GD], dx)

    arrived(PM, rs_one.at[R_PM])
    arrived(gf_out, rs_one.at[R_GF])
    arrived(gs_out, rs_one.at[R_GS])
    arrived(gd_out, rs_one.at[R_GD])
    assert next(count) <= FBASE
    for copy in pending:
        copy.wait_send()
    for k in range(CHUNKS):
        for to in range(1, 4):
            @pl.when(y < to)
            def _():
                copy_f(k, to).wait_send()
        for to in range(3):
            @pl.when(y > to)
            def _():
                copy_b(k, to).wait_send()


def settle(gf, gs, gd, pm, gf_out, gs_out, gd_out, gim_out, gom_out, sem):
    copies = [
        pltpu.make_async_copy(a, b, sem.at[i])
        for i, (a, b) in enumerate(((gf, gf_out), (gs, gs_out), (gd, gd_out)))
    ]
    for copy in copies:
        copy.start()
    for g in range(2):
        gim_out[:, g, :] = pm[g, 0, 0].astype(F32) + pm[g, 1, 0].astype(F32)
        gom_out[:, g, :] = pm[g, 0, 1].astype(F32) + pm[g, 1, 1].astype(F32)
    for copy in copies:
        copy.wait()


def per_device(features, step_size, log_decay, input_map, output_map, segment, sent_grad):
    feat = jnp.transpose(features[0], (1, 2, 0)).reshape(64 * W, T)
    step = step_size[0].T
    dec = log_decay[0].T
    grad = sent_grad[0]
    any_ = pl.BlockSpec(memory_space=pltpu.HBM)
    vmem = pl.BlockSpec(memory_space=pltpu.VMEM)
    V_ = pltpu.VMEM
    scratch = [
        V_((CHUNKS, ROW, CW, T), BF16),
        V_((CHUNKS, ROW, CW, T), BF16),
        V_((CHUNKS, ROW, T, CW), BF16),
        V_((CHUNKS, ROW, CW, T), BF16),
        V_((CHUNKS, ROW, CW, T), BF16),
        V_((ROW, 2, T, N), BF16),
        V_((ROW, HEADS, T), F32),
        V_((ROW, HEADS, T), F32),
        V_((ROW, 8, T), F32),
        V_((8, T), F32),
        V_((ROW, HEADS, T), F32),
        V_((ROW, T, T), F32),
        V_((ROW, HEADS, T), F32),
        V_((ROW, HEADS, T), F32),
        V_((ROW, HEADS, T), F32),
        V_((ROW, HEADS, N), F32),
        V_((ROW + 1, HEADS, N), F32),
        V_((ROW, HEADS, N), F32),
        V_((ROW, T, T), F32),
        V_((ROW, T, T), F32),
        V_((ROW, T, T), F32),
        V_((CHUNKS, ROW + 1, CW, N), F32),
        V_((CHUNKS, ROW + 1, CW, N), F32),
        V_((CHUNKS, ROW, CW, T), F32),
        V_((ROW, T, T), F32),
        V_((ROW, HEADS, T), F32),
        V_((ROW, T, T), F32),
        V_((ROW, HEADS, T), F32),
        V_((ROW, HEADS, T), F32),
        V_((ROW, HEADS, T), F32),
        V_((CHUNKS, 3, CW, N), BF16),
        V_((CHUNKS, 3, CW, N), BF16),
        V_((CHUNKS, CW, N), BF16),
        V_((CHUNKS, CW, N), BF16),
        V_((CW, N), F32),
        V_((CW, N), F32),
        V_((CHUNKS, ROW, CW, N), BF16),
        V_((3, HEADS, N), F32),
        V_((3, HEADS, N), F32),
        V_((4, HEADS, T), F32),
        V_((HEADS, T), F32),
        V_((ROW, T, N), F32),
        V_((ROW, T, N), F32),
        V_((ROW, 2, T, N), BF16),
        V_((CHUNKS, ROW, CW, T), BF16),
        V_((ROW, HEADS, T), F32),
        V_((ROW, HEADS, T), F32),
        V_((1, T), jnp.int32),
        V_((8, T), F32),
        V_((2, T, 2, N), BF16),
        V_((2, 2, T, N), BF16),
        pltpu.SemaphoreType.DMA((FBASE + 6 * CHUNKS,)),
        pltpu.SemaphoreType.DMA((13,)),
        pltpu.SemaphoreType.DMA((CHUNKS,)),
        pltpu.SemaphoreType.DMA((CHUNKS,)),
        pltpu.SemaphoreType.DMA((CHUNKS,)),
        pltpu.SemaphoreType.DMA((CHUNKS, 3)),
        pltpu.SemaphoreType.DMA((CHUNKS, 3)),
        pltpu.SemaphoreType.REGULAR,
    ]
    gf, gs, gd, pm = pl.pallas_call(
        kernel,
        out_shape=(
            jax.ShapeDtypeStruct((64 * W, T), BF16),
            jax.ShapeDtypeStruct((64, T), F32),
            jax.ShapeDtypeStruct((64, T), F32),
            jax.ShapeDtypeStruct((2, 2, 2, T, N), BF16),
        ),
        in_specs=[any_] * 7,
        out_specs=(any_, any_, any_, any_),
        scratch_shapes=scratch,
        compiler_params=pltpu.CompilerParams(
            collective_id=0, has_side_effects=True, vmem_limit_bytes=60 * 2**20
        ),
        name="ssd_backward",
    )(feat, step, dec, input_map[0], output_map[0], segment, grad)
    gf, gs, gd, gim, gom = pl.pallas_call(
        settle,
        out_shape=(
            jax.ShapeDtypeStruct((64 * W, T), BF16),
            jax.ShapeDtypeStruct((64, T), F32),
            jax.ShapeDtypeStruct((64, T), F32),
            jax.ShapeDtypeStruct((T, 2, N), F32),
            jax.ShapeDtypeStruct((T, 2, N), F32),
        ),
        in_specs=[any_, any_, any_, vmem],
        out_specs=(vmem,) * 5,
        scratch_shapes=[pltpu.SemaphoreType.DMA((3,))],
        name="settle",
    )(gf, gs, gd, pm)
    return (
        jnp.transpose(gf.reshape(64, W, T), (2, 0, 1))[None],
        gs.T[None],
        gd.T[None],
        gim[None],
        gom[None],
    )


def solution(mesh):
    placed = (
        P("section", "seq", "head", None),
        P("section", "seq", "head"),
        P("section", "seq", "head"),
        P("section", "seq", "head", None),
        P("section", "seq", "head", None),
        P("section", "seq"),
        P("section", ("seq", "head"), None),
    )
    return jax.shard_map(
        per_device,
        mesh=mesh,
        in_specs=placed,
        out_specs=(
            P("section", "seq", "head", None),
            P("section", "seq", "head"),
            P("section", "seq", "head"),
            P("section", "seq", "head", None),
            P("section", "seq", "head", None),
        ),
        check_vma=False,
    )
```

time: 81 us -> 64.3 us (0.79)
  the two profiles are of different devices: /device:TPU:1 before, /device:TPU:248 now
where the time goes in v2:
time: 64.3 us; the launch traced here: 64.1 us
  Pallas kernels  63.5 us (99%)
    pallas_call x1, Pallas kernels, per_device(): pl.pallas_call(kernel, out_shape=(jax.ShapeDtypeStruct((64 * W, T), BF16)...  60 us
    pallas_call x1, Pallas kernels, per_device(): pl.pallas_call(settle, out_shape=(jax.ShapeDtypeStruct((64 * W, T), BF16)...  3.45 us

profile of v2, /device:TPU:248, one launch (start us, length us, event | category | flops | bytes accessed | tf_op | source)
XLA Modules:
  0.0 64.1 jit_solution(4974508786619362439)
XLA Ops:
  0.6 60.0 %ssd_backward.1 = (bf16[4096,128]{1,0:T(8,128)(2,1)}, f32[64,128]{1,0:T(8,128)}, f32[64,128]{1,0:T(8,128)}, bf16[2,2,2,128,256]{4,3,2,1,0:T(8,128)(2,1)}) custom-call(bf16[4096,128]{1,0:T(8,128)(2,1)} %bitcast.27, f32[64,128]{1,0:T(8,128)} %bitcast.31, f32[64,128]{1,0:T(8,128)} %bitcast.32, bf16[128,2,256]{2,1,0:T(2,128)(2,1)} %bitcast.29, ...), custom_call_target="tpu_custom_call" | custom-call | tf_op jit(solution)/shard_map/ssd_backward/pallas_call | solution.py:544
  60.7 3.5 %settle.1 = (bf16[4096,128]{1,0:T(8,128)(2,1)}, f32[64,128]{1,0:T(8,128)}, f32[64,128]{1,0:T(8,128)}, f32[128,2,256]{2,1,0:T(2,128)}, f32[128,2,256]{2,1,0:T(2,128)}) custom-call(bf16[4096,128]{1,0:T(8,128)(2,1)} %get-tuple-element.14.gf, f32[64,128]{1,0:T(8,128)} %get-tuple-element.15.gs, f32[64,128]{1,0:T(8,128)} %get-tuple-element.16.gd, ...), custom_call_target="tpu_custom_call" | custom-call | tf_op jit(solution)/shard_map/settle/pallas_call | solution.py:560

commit v3 on v2

--- a/solution.py
+++ b/solution.py
@@ -20,6 +20,7 @@
 CHUNKS = 8
 HC = HEADS // CHUNKS
 WINDOW = 3
+PIECES = 4
 LAG = 2
 CW = HC * W
 FBASE = 40 + 8 * CHUNKS
@@ -56,7 +57,7 @@
     L, LT, HW, TW, STW, DB, CF, CB, CM, MASK, PRE,
     PF, PB, VI, WS, CK, RK, U, V, B4,
     RF, RB, ES, GS, EA, GA, EB, COF, COB, RDEC, ROWD,
-    GIM, GOM, PMS, GF, GSS, GDS, SEGI, SEGF, RAW, MAPS,
+    GIM, GOM, PMS, GF, GSS, GDS, SEGI, SEGF, RAW, MAPS, MAPT,
     ssem, rs_one, ss_grad, rs_feat, rs_grad, rs_f, rs_b, ready,
 ):
     s = lax.axis_index("section")
@@ -237,7 +238,9 @@
         send(ROWD, RDEC.at[y], rs_one.at[R_RD], place(s, y + dy, x, c))
     arrived(MAP, rs_one.at[R_MAP])
     for b in range(ROW):
-        CM[b] = dot_nt(MAP[b, 1], MAP[b, 0])
+        MAPT[b, 0] = jnp.transpose(MAP[b, 0])
+        MAPT[b, 1] = jnp.transpose(MAP[b, 1])
+        CM[b] = dot(MAP[b, 1], MAPT[b, 0])
         WS[b] = jnp.zeros((T, T), F32)
         RK[b] = jnp.zeros((T, T), F32)
         GIM[b] = jnp.zeros((T, N), F32)
@@ -351,7 +354,7 @@
             RK[b] = sums
             return carry
 
-        lax.fori_loop(0, ROW, one_block, 0)
+        lax.fori_loop(0, ROW, one_block, 0, unroll=4)
 
     def row_factors():
         arrived(RDEC, rs_one.at[R_RD])
@@ -372,20 +375,20 @@
         def one_block(b, carry):
             eb = (PF[k, b] + scaled(EA[...], heads_of(CF, b, k))).astype(BF16)
             EB[k, b] = eb
-            seen = dot_nt(eb, MAP[b, 1])
+            seen = dot(eb, MAPT[b, 1])
             hs = slice(HC * k, HC * (k + 1))
             U[b, hs, :] = heads_of(HW, b, k) * jnp.sum(by_head(GRT[k, b].astype(F32) * seen), axis=1)
             GOM[b] += dot_tn(GHW[k, b], eb)
             return carry
 
-        lax.fori_loop(0, ROW, one_block, 0)
+        lax.fori_loop(0, ROW, one_block, 0, unroll=4)
 
     def finish_b(k):
         enter_b(k)
 
         def one_block(b, carry):
             gb = (PB[k, b + 1] + scaled(GA[...], heads_of(CB, b, k))).astype(BF16)
-            lift = dot_nt(gb, MAP[b, 0])
+            lift = dot(gb, MAPT[b, 0])
             val = VI[k, b] + scaled(lift, heads_of(TW, b, k))
             GF[k, b] = scaled(val, heads_of(STEP, b, k)).astype(BF16)
             hs = slice(HC * k, HC * (k + 1))
@@ -395,7 +398,7 @@
             GIM[b] += dot_tn(XW[k, b], gb)
             return carry
 
-        lax.fori_loop(0, ROW, one_block, 0)
+        lax.fori_loop(0, ROW, one_block, 0, unroll=4)
         for dx in range(4):
             rows = pl.ds(pl.multiple_of((first_head + HC * k) * W, CW), CW)
             to_worker(GF.at[k, workers[dx]], gf_out.at[rows], rs_one.at[R_GF], dx)
@@ -458,17 +461,35 @@
                 copy_b(k, to).wait_send()
 
 
-def settle(gf, gs, gd, pm, gf_out, gs_out, gd_out, gim_out, gom_out, sem):
-    copies = [
-        pltpu.make_async_copy(a, b, sem.at[i])
-        for i, (a, b) in enumerate(((gf, gf_out), (gs, gs_out), (gd, gd_out)))
-    ]
-    for copy in copies:
+def settle(
+    gf, gs, gd, pm, gf_out, gs_out, gd_out, gim_out, gom_out,
+    held, steps, maps, sums, sem_in, sem_out,
+):
+    size = 64 * W // PIECES
+    reads, writes = [], []
+    for g in range(2):
+        reads.append(pltpu.make_async_copy(pm.at[g], maps.at[g], sem_in.at[g]))
+    for i in range(PIECES):
+        rows = pl.ds(i * size, size)
+        reads.append(pltpu.make_async_copy(gf.at[rows], held.at[rows], sem_in.at[2 + i]))
+        writes.append(pltpu.make_async_copy(held.at[rows], gf_out.at[rows], sem_out.at[i]))
+    for i, (a, b) in enumerate(((gs, gs_out), (gd, gd_out))):
+        reads.append(pltpu.make_async_copy(a, steps.at[i], sem_in.at[2 + PIECES + i]))
+        writes.append(pltpu.make_async_copy(steps.at[i], b, sem_out.at[PIECES + i]))
+    for copy in reads:
         copy.start()
     for g in range(2):
-        gim_out[:, g, :] = pm[g, 0, 0].astype(F32) + pm[g, 1, 0].astype(F32)
-        gom_out[:, g, :] = pm[g, 0, 1].astype(F32) + pm[g, 1, 1].astype(F32)
-    for copy in copies:
+        reads[g].wait()
+        for m in range(2):
+            sums[m, :, g, :] = maps[g, 0, m].astype(F32) + maps[g, 1, m].astype(F32)
+    for m, out in enumerate((gim_out, gom_out)):
+        copy = pltpu.make_async_copy(sums.at[m], out, sem_out.at[PIECES + 2 + m])
+        copy.start()
+        writes.append(copy)
+    for i in range(PIECES + 2):
+        reads[2 + i].wait()
+        writes[i].start()
+    for copy in writes:
         copy.wait()
 
 
@@ -478,7 +499,6 @@
     dec = log_decay[0].T
     grad = sent_grad[0]
     any_ = pl.BlockSpec(memory_space=pltpu.HBM)
-    vmem = pl.BlockSpec(memory_space=pltpu.VMEM)
     V_ = pltpu.VMEM
     scratch = [
         V_((CHUNKS, ROW, CW, T), BF16),
@@ -532,6 +552,7 @@
         V_((8, T), F32),
         V_((2, T, 2, N), BF16),
         V_((2, 2, T, N), BF16),
+        V_((ROW, 2, N, T), BF16),
         pltpu.SemaphoreType.DMA((FBASE + 6 * CHUNKS,)),
         pltpu.SemaphoreType.DMA((13,)),
         pltpu.SemaphoreType.DMA((CHUNKS,)),
@@ -566,9 +587,17 @@
             jax.ShapeDtypeStruct((T, 2, N), F32),
             jax.ShapeDtypeStruct((T, 2, N), F32),
         ),
-        in_specs=[any_, any_, any_, vmem],
-        out_specs=(vmem,) * 5,
-        scratch_shapes=[pltpu.SemaphoreType.DMA((3,))],
+        in_specs=[any_] * 4,
+        out_specs=(any_,) * 5,
+        scratch_shapes=[
+            V_((64 * W, T), BF16),
+            V_((2, 64, T), F32),
+            V_((2, 2, 2, T, N), BF16),
+            V_((2, T, 2, N), F32),
+            pltpu.SemaphoreType.DMA((PIECES + 4,)),
+            pltpu.SemaphoreType.DMA((PIECES + 4,)),
+        ],
+        compiler_params=pltpu.CompilerParams(vmem_limit_bytes=60 * 2**20),
         name="settle",
     )(gf, gs, gd, pm)
     return (

time: 64.3 us -> 60.7 us (0.944)
  the two profiles are of different devices: /device:TPU:248 before, /device:TPU:1 now
where the time goes in v3:
time: 60.7 us; the launch traced here: 59.5 us
  Pallas kernels  58.7 us (97%)
  between operations  0.8 us (1%)
    pallas_call x1, Pallas kernels, per_device(): pl.pallas_call(kernel, out_shape=(jax.ShapeDtypeStruct((64 * W, T), BF16)...  56.3 us
    pallas_call x1, Pallas kernels, per_device(): pl.pallas_call(settle, out_shape=(jax.ShapeDtypeStruct((64 * W, T), BF16)...  2.42 us

profile of v3, /device:TPU:1, one launch (start us, length us, event | category | flops | bytes accessed | tf_op | source)
XLA Modules:
  0.0 59.5 jit_solution(16880924563253584532)
XLA Ops:
  0.6 56.3 %ssd_backward.1 = (bf16[4096,128]{1,0:T(8,128)(2,1)}, f32[64,128]{1,0:T(8,128)}, f32[64,128]{1,0:T(8,128)}, bf16[2,2,2,128,256]{4,3,2,1,0:T(8,128)(2,1)}) custom-call(bf16[4096,128]{1,0:T(8,128)(2,1)} %bitcast.27, f32[64,128]{1,0:T(8,128)} %bitcast.31, f32[64,128]{1,0:T(8,128)} %bitcast.32, bf16[128,2,256]{2,1,0:T(2,128)(2,1)} %bitcast.29, ...), custom_call_target="tpu_custom_call" | custom-call | tf_op jit(solution)/shard_map/ssd_backward/pallas_call | solution.py:565
  56.9 2.4 %settle.1 = (bf16[4096,128]{1,0:T(8,128)(2,1)}, f32[64,128]{1,0:T(8,128)}, f32[64,128]{1,0:T(8,128)}, f32[128,2,256]{2,1,0:T(2,128)}, f32[128,2,256]{2,1,0:T(2,128)}) custom-call(bf16[4096,128]{1,0:T(8,128)(2,1)} %get-tuple-element.14.gf, f32[64,128]{1,0:T(8,128)} %get-tuple-element.15.gs, f32[64,128]{1,0:T(8,128)} %get-tuple-element.16.gd, ...), custom_call_target="tpu_custom_call" | custom-call | tf_op jit(solution)/shard_map/settle/pallas_call | solution.py:581

commit v4 on v3

--- a/solution.py
+++ b/solution.py
@@ -23,7 +23,7 @@
 PIECES = 4
 LAG = 2
 CW = HC * W
-FBASE = 40 + 8 * CHUNKS
+FBASE = 48 + 8 * CHUNKS
 
 
 def dot(a, b, precision=None):
@@ -57,7 +57,7 @@
     L, LT, HW, TW, STW, DB, CF, CB, CM, MASK, PRE,
     PF, PB, VI, WS, CK, RK, U, V, B4,
     RF, RB, ES, GS, EA, GA, EB, COF, COB, RDEC, ROWD,
-    GIM, GOM, PMS, GF, GSS, GDS, SEGI, SEGF, RAW, MAPS, MAPT,
+    GIM, GOM, PMS, PX, PO, GF, GSS, GDS, SEGI, SEGF, RAW, MAPS, MAPT,
     ssem, rs_one, ss_grad, rs_feat, rs_grad, rs_f, rs_b, ready,
 ):
     s = lax.axis_index("section")
@@ -65,8 +65,10 @@
     c = lax.axis_index("head")
     y = q // 4
     x = lax.rem(q, 4)
-    first_head = 16 * x
-    R_SEG, R_STEP, R_DEC, R_MAP, R_PREV, R_GF, R_GS, R_GD, R_PM, R_RD, R_A, R_B, R_C = range(13)
+    co = x // 2
+    half = lax.rem(x, 2)
+    first_head = 32 * half + 16 * c
+    R_SEG, R_STEP, R_DEC, R_MAP, R_PREV, R_GF, R_GS, R_GD, R_PM, R_RD, R_A, R_B, R_C, R_CROSS, R_SUM = range(15)
 
     barrier = pltpu.get_barrier_semaphore()
     load_seg = pltpu.make_async_copy(seg, SEGI, rs_one.at[R_A])
@@ -111,13 +113,35 @@
     pending = []
     count = itertools.count()
 
-    def send(src, dst, rsem, target):
+    def send(src, dst, rsem, target, own=None):
         copy = pltpu.make_async_remote_copy(
             src_ref=src, dst_ref=dst, send_sem=ssem.at[next(count)], recv_sem=rsem,
             device_id=target, device_id_type=MESH,
         )
-        copy.start()
-        pending.append(copy)
+        if own is None:
+            copy.start()
+            pending.append((None, copy))
+        else:
+            away = jnp.logical_not(own)
+
+            @pl.when(own)
+            def _():
+                pltpu.make_async_copy(src, dst, rsem).start()
+
+            @pl.when(away)
+            def _():
+                copy.start()
+
+            pending.append((away, copy))
+
+    def sent(sends):
+        for away, copy in sends:
+            if away is None:
+                copy.wait_send()
+            else:
+                @pl.when(away)
+                def _(copy=copy):
+                    copy.wait_send()
 
     def arrived(ref, sem):
         pltpu.make_async_copy(ref, ref, sem).wait()
@@ -125,27 +149,31 @@
     pltpu.make_async_copy(SEGF, SEG.at[x], rs_one.at[R_SEG]).start()
     for dx in range(1, 4):
         send(SEGF, SEG.at[x], rs_one.at[R_SEG], place(s, y, x + dx, c))
-    workers = [lax.rem(x + dx, 4) for dx in range(4)]
-
-    def to_worker(src, dst, rsem, dx):
-        if dx == 0:
-            pltpu.make_async_copy(src, dst, rsem).start()
-        else:
-            send(src, dst, rsem, place(s, y, workers[dx], c))
-
-    for dx in range(4):
-        rows = pl.ds(pl.multiple_of(16 * workers[dx], 16), 16)
-        to_worker(step.at[rows], STEP.at[x], rs_one.at[R_STEP], dx)
-        to_worker(dec.at[rows], DEC.at[x], rs_one.at[R_DEC], dx)
-    for dx in range(4):
-        to_worker(MAPS.at[workers[dx] // 2], MAP.at[x], rs_one.at[R_MAP], dx)
+    chips = [lax.rem(x + dx, 4) for dx in range(4)]
+    workers = []
+    for gl in range(2):
+        for dc in range(2):
+            xw = 2 * c + gl
+            own = (xw == x) if dc == 0 else None
+            workers.append((gl, xw, lax.rem(c + dc, 2), own))
+
+    def to_owner(src, dst, rsem, dx):
+        own = (c == co) if dx == 0 else None
+        send(src, dst, rsem, place(s, y, chips[dx], co), own)
+
+    for gl, xw, cw, own in workers:
+        rows = pl.ds(pl.multiple_of(32 * gl + 16 * cw, 16), 16)
+        send(step.at[rows], STEP.at[x], rs_one.at[R_STEP], place(s, y, xw, cw), own)
+        send(dec.at[rows], DEC.at[x], rs_one.at[R_DEC], place(s, y, xw, cw), own)
+    for gl, xw, cw, own in workers:
+        send(MAPS.at[gl, cw], MAP.at[cw, x], rs_one.at[R_MAP], place(s, y, xw, cw), own)
     feat_sends = {}
 
     def issue_feat(k):
         before = len(pending)
-        for dx in range(4):
-            rows = pl.ds(pl.multiple_of((16 * workers[dx] + HC * k) * W, CW), CW)
-            to_worker(feat.at[rows], XT.at[k, x], rs_feat.at[k], dx)
+        for gl, xw, cw, own in workers:
+            rows = pl.ds(pl.multiple_of((32 * gl + 16 * cw + HC * k) * W, CW), CW)
+            send(feat.at[rows], XT.at[k, x], rs_feat.at[k], place(s, y, xw, cw), own)
         feat_sends[k] = pending[before:]
         del pending[before:]
 
@@ -154,7 +182,7 @@
             for dc in range(2):
                 xw = lax.rem(x + dx, 4)
                 cw = lax.rem(c + dc, 2)
-                cols = pl.ds(pl.multiple_of((64 * cw + 16 * xw + HC * k) * W, CW), CW)
+                cols = pl.ds(pl.multiple_of((32 * xw + 16 * cw + HC * k) * W, CW), CW)
                 pltpu.make_async_remote_copy(
                     src_ref=grad.at[:, cols],
                     dst_ref=GRN.at[k, x, pl.ds(pl.multiple_of(64 * c, 64), 64), :],
@@ -165,8 +193,7 @@
                 ).start()
 
     def gone(k):
-        for copy in feat_sends[k]:
-            copy.wait_send()
+        sent(feat_sends[k])
         arrived(grad.at[:, pl.ds(0, 8 * CW)], ss_grad.at[k])
 
     for k in range(WINDOW):
@@ -236,11 +263,13 @@
     pltpu.make_async_copy(ROWD, RDEC.at[y], rs_one.at[R_RD]).start()
     for dy in range(1, 4):
         send(ROWD, RDEC.at[y], rs_one.at[R_RD], place(s, y + dy, x, c))
-    arrived(MAP, rs_one.at[R_MAP])
+    arrived(MAP.at[c], rs_one.at[R_MAP])
+    send(MAP.at[c], MAP.at[c], rs_one.at[R_CROSS], place(s, y, x, c + 1))
+    arrived(MAP.at[1 - c], rs_one.at[R_CROSS])
     for b in range(ROW):
-        MAPT[b, 0] = jnp.transpose(MAP[b, 0])
-        MAPT[b, 1] = jnp.transpose(MAP[b, 1])
-        CM[b] = dot(MAP[b, 1], MAPT[b, 0])
+        MAPT[b, 0] = jnp.transpose(MAP[0, b])
+        MAPT[b, 1] = jnp.transpose(MAP[1, b])
+        CM[b] = dot(MAP[1, b], MAPT[b, 0])
         WS[b] = jnp.zeros((T, T), F32)
         RK[b] = jnp.zeros((T, T), F32)
         GIM[b] = jnp.zeros((T, N), F32)
@@ -274,7 +303,7 @@
         for b in range(ROW):
             xw = scaled(XT[k, b].astype(F32), heads_of(STW, b, k)).astype(BF16)
             XW[k, b] = xw
-            total = scaled(total, heads_of(DB, b, k)) + dot(xw, MAP[b, 0])
+            total = scaled(total, heads_of(DB, b, k)) + dot(xw, MAP[0, b])
             PF[k, b + 1] = total
         ES[k] = total.astype(BF16)
         for to in range(1, 4):
@@ -291,7 +320,7 @@
             GRT[k, b] = gt
             gh = scaled(gt.astype(F32), heads_of(HW, b, k)).astype(BF16)
             GHW[k, b] = gh
-            total = scaled(total, heads_of(DB, b, k)) + dot(gh, MAP[b, 1])
+            total = scaled(total, heads_of(DB, b, k)) + dot(gh, MAP[1, b])
             PB[k, b] = total
         GS[k] = total.astype(BF16)
         for to in range(3):
@@ -401,11 +430,56 @@
         lax.fori_loop(0, ROW, one_block, 0, unroll=4)
         for dx in range(4):
             rows = pl.ds(pl.multiple_of((first_head + HC * k) * W, CW), CW)
-            to_worker(GF.at[k, workers[dx]], gf_out.at[rows], rs_one.at[R_GF], dx)
-
-    def send_map(m):
+            to_owner(GF.at[k, chips[dx]], gf_out.at[rows], rs_one.at[R_GF], dx)
+
+    def send_map(m, first, second):
+        @pl.when(c != m)
+        def _():
+            for b in range(ROW):
+                PMS[b] = (first[b] + second(b)).astype(BF16)
+            cross[m].start()
+
+        @pl.when(c == m)
+        def _():
+            for b in range(ROW):
+                first[b] = first[b] + second(b)
+            arrived(PX, rs_one.at[R_SUM])
+            for b in range(ROW):
+                PO[b] = (first[b] + PX[b].astype(F32)).astype(BF16)
+            for dx in range(4):
+                if dx == 0:
+                    @pl.when(c == co)
+                    def _():
+                        pltpu.make_async_copy(PO.at[x], PM.at[half, m], rs_one.at[R_PM]).start()
+
+                    @pl.when(c != co)
+                    def _():
+                        summed[m][0].start()
+                else:
+                    summed[m][dx].start()
+
+    cross, summed = [], []
+    for m in range(2):
+        cross.append(
+            pltpu.make_async_remote_copy(
+                src_ref=PMS, dst_ref=PX, send_sem=ssem.at[next(count)], recv_sem=rs_one.at[R_SUM],
+                device_id=place(s, y, x, c + 1), device_id_type=MESH,
+            )
+        )
+        pending.append((c != m, cross[m]))
+        summed.append([])
         for dx in range(4):
-            to_worker(PMS.at[workers[dx], m], PM.at[x // 2, lax.rem(x, 2), m], rs_one.at[R_PM], dx)
+            summed[m].append(
+                pltpu.make_async_remote_copy(
+                    src_ref=PO.at[chips[dx]], dst_ref=PM.at[half, m], send_sem=ssem.at[next(count)],
+                    recv_sem=rs_one.at[R_PM], device_id=place(s, y, chips[dx], co),
+                    device_id_type=MESH,
+                )
+            )
+            going = c == m
+            if dx == 0:
+                going = jnp.logical_and(going, c != co)
+            pending.append((going, summed[m][dx]))
 
     for k in range(CHUNKS):
         local_states(k)
@@ -423,13 +497,9 @@
     for k in range(CHUNKS - LAG, CHUNKS):
         finish_f(k)
         if k + 1 == CHUNKS:
-            for b in range(ROW):
-                PMS[b, 1] = (GOM[b] + dot(WS[b].astype(BF16), MAP[b, 0])).astype(BF16)
-            send_map(1)
+            send_map(1, GOM, lambda b: dot(WS[b].astype(BF16), MAP[0, b]))
         finish_b(k)
-    for b in range(ROW):
-        PMS[b, 0] = (GIM[b] + dot_tn(WS[b].astype(BF16), MAP[b, 1])).astype(BF16)
-    send_map(0)
+    send_map(0, GIM, lambda b: dot_tn(WS[b].astype(BF16), MAP[1, b]))
 
     for b in range(ROW):
         row_sums = jnp.transpose(RK[b])[0:HEADS, :]
@@ -440,16 +510,15 @@
         GDS[b] = chain + HW[b] * TW[b] * B4[b]
     for dx in range(4):
         rows = pl.ds(pl.multiple_of(first_head, 16), 16)
-        to_worker(GSS.at[workers[dx]], gs_out.at[rows], rs_one.at[R_GS], dx)
-        to_worker(GDS.at[workers[dx]], gd_out.at[rows], rs_one.at[R_GD], dx)
+        to_owner(GSS.at[chips[dx]], gs_out.at[rows], rs_one.at[R_GS], dx)
+        to_owner(GDS.at[chips[dx]], gd_out.at[rows], rs_one.at[R_GD], dx)
 
     arrived(PM, rs_one.at[R_PM])
     arrived(gf_out, rs_one.at[R_GF])
     arrived(gs_out, rs_one.at[R_GS])
     arrived(gd_out, rs_one.at[R_GD])
     assert next(count) <= FBASE
-    for copy in pending:
-        copy.wait_send()
+    sent(pending)
     for k in range(CHUNKS):
         for to in range(1, 4):
             @pl.when(y < to)
@@ -481,7 +550,7 @@
     for g in range(2):
         reads[g].wait()
         for m in range(2):
-            sums[m, :, g, :] = maps[g, 0, m].astype(F32) + maps[g, 1, m].astype(F32)
+            sums[m, :, g, :] = maps[g, m].astype(F32)
     for m, out in enumerate((gim_out, gom_out)):
         copy = pltpu.make_async_copy(sums.at[m], out, sem_out.at[PIECES + 2 + m])
         copy.start()
@@ -506,7 +575,7 @@
         V_((CHUNKS, ROW, T, CW), BF16),
         V_((CHUNKS, ROW, CW, T), BF16),
         V_((CHUNKS, ROW, CW, T), BF16),
-        V_((ROW, 2, T, N), BF16),
+        V_((2, ROW, T, N), BF16),
         V_((ROW, HEADS, T), F32),
         V_((ROW, HEADS, T), F32),
         V_((ROW, 8, T), F32),
@@ -544,7 +613,9 @@
         V_((HEADS, T), F32),
         V_((ROW, T, N), F32),
         V_((ROW, T, N), F32),
-        V_((ROW, 2, T, N), BF16),
+        V_((ROW, T, N), BF16),
+        V_((ROW, T, N), BF16),
+        V_((ROW, T, N), BF16),
         V_((CHUNKS, ROW, CW, T), BF16),
         V_((ROW, HEADS, T), F32),
         V_((ROW, HEADS, T), F32),
@@ -554,7 +625,7 @@
         V_((2, 2, T, N), BF16),
         V_((ROW, 2, N, T), BF16),
         pltpu.SemaphoreType.DMA((FBASE + 6 * CHUNKS,)),
-        pltpu.SemaphoreType.DMA((13,)),
+        pltpu.SemaphoreType.DMA((15,)),
         pltpu.SemaphoreType.DMA((CHUNKS,)),
         pltpu.SemaphoreType.DMA((CHUNKS,)),
         pltpu.SemaphoreType.DMA((CHUNKS,)),
@@ -568,7 +639,7 @@
             jax.ShapeDtypeStruct((64 * W, T), BF16),
             jax.ShapeDtypeStruct((64, T), F32),
             jax.ShapeDtypeStruct((64, T), F32),
-            jax.ShapeDtypeStruct((2, 2, 2, T, N), BF16),
+            jax.ShapeDtypeStruct((2, 2, T, N), BF16),
         ),
         in_specs=[any_] * 7,
         out_specs=(any_, any_, any_, any_),
@@ -592,7 +663,7 @@
         scratch_shapes=[
             V_((64 * W, T), BF16),
             V_((2, 64, T), F32),
-            V_((2, 2, 2, T, N), BF16),
+            V_((2, 2, T, N), BF16),
             V_((2, T, 2, N), F32),
             pltpu.SemaphoreType.DMA((PIECES + 4,)),
             pltpu.SemaphoreType.DMA((PIECES + 4,)),

time: 60.7 us -> 57 us (0.939); the launches traced: 59.5 us -> 56.6 us
  Pallas kernels: 58.7 us -> 55.8 us
    pallas_call x1, Pallas kernels: 56.3 us -> 53.5 us  [per_device(): pl.pallas_call(kernel, out_shape=(jax.ShapeDtypeStruct((64 * W, T), BF16)...]
where the time goes in v4:
time: 57 us; the launch traced here: 56.6 us
  Pallas kernels  55.8 us (98%)
  between operations  0.8 us (1%)
    pallas_call x1, Pallas kernels, per_device(): pl.pallas_call(kernel, out_shape=(jax.ShapeDtypeStruct((64 * W, T), BF16)...  53.5 us
    pallas_call x1, Pallas kernels, per_device(): pl.pallas_call(settle, out_shape=(jax.ShapeDtypeStruct((64 * W, T), BF16)...  2.35 us

profile of v4, /device:TPU:1, one launch (start us, length us, event | category | flops | bytes accessed | tf_op | source)
XLA Modules:
  0.0 56.6 jit_solution(17556617954629214752)
XLA Ops:
  0.6 53.5 %ssd_backward.1 = (bf16[4096,128]{1,0:T(8,128)(2,1)}, f32[64,128]{1,0:T(8,128)}, f32[64,128]{1,0:T(8,128)}, bf16[2,2,128,256]{3,2,1,0:T(8,128)(2,1)}) custom-call(bf16[4096,128]{1,0:T(8,128)(2,1)} %bitcast.27, f32[64,128]{1,0:T(8,128)} %bitcast.31, f32[64,128]{1,0:T(8,128)} %bitcast.32, bf16[128,2,256]{2,1,0:T(2,128)(2,1)} %bitcast.29, ...), custom_call_target="tpu_custom_call" | custom-call | tf_op jit(solution)/shard_map/ssd_backward/pallas_call | solution.py:636
  54.1 2.4 %settle.1 = (bf16[4096,128]{1,0:T(8,128)(2,1)}, f32[64,128]{1,0:T(8,128)}, f32[64,128]{1,0:T(8,128)}, f32[128,2,256]{2,1,0:T(2,128)}, f32[128,2,256]{2,1,0:T(2,128)}) custom-call(bf16[4096,128]{1,0:T(8,128)(2,1)} %get-tuple-element.14.gf, f32[64,128]{1,0:T(8,128)} %get-tuple-element.15.gs, f32[64,128]{1,0:T(8,128)} %get-tuple-element.16.gd, ...), custom_call_target="tpu_custom_call" | custom-call | tf_op jit(solution)/shard_map/settle/pallas_call | solution.py:652

commit v5 on v4

--- a/solution.py
+++ b/solution.py
@@ -19,9 +19,9 @@
 HEADS = 16
 CHUNKS = 8
 HC = HEADS // CHUNKS
-WINDOW = 3
+WINDOW = 4
 PIECES = 4
-LAG = 2
+LAG = 3
 CW = HC * W
 FBASE = 48 + 8 * CHUNKS
 
@@ -432,20 +432,19 @@
             rows = pl.ds(pl.multiple_of((first_head + HC * k) * W, CW), CW)
             to_owner(GF.at[k, chips[dx]], gf_out.at[rows], rs_one.at[R_GF], dx)
 
-    def send_map(m, first, second):
+    def part_of_map(m, total):
         @pl.when(c != m)
         def _():
             for b in range(ROW):
-                PMS[b] = (first[b] + second(b)).astype(BF16)
+                PMS[b] = total[b].astype(BF16)
             cross[m].start()
 
+    def sum_of_map(m, total):
         @pl.when(c == m)
         def _():
-            for b in range(ROW):
-                first[b] = first[b] + second(b)
             arrived(PX, rs_one.at[R_SUM])
             for b in range(ROW):
-                PO[b] = (first[b] + PX[b].astype(F32)).astype(BF16)
+                PO[b] = (total[b] + PX[b].astype(F32)).astype(BF16)
             for dx in range(4):
                 if dx == 0:
                     @pl.when(c == co)
@@ -491,23 +490,30 @@
         intra(k)
         if k == 0:
             row_factors()
+        if k + 1 == CHUNKS:
+            for b in range(ROW):
+                w = WS[b].astype(BF16)
+                GOM[b] += dot(w, MAP[0, b])
+                GIM[b] += dot_tn(w, MAP[1, b])
         if k >= LAG:
             finish_f(k - LAG)
             finish_b(k - LAG)
     for k in range(CHUNKS - LAG, CHUNKS):
         finish_f(k)
         if k + 1 == CHUNKS:
-            send_map(1, GOM, lambda b: dot(WS[b].astype(BF16), MAP[0, b]))
+            part_of_map(1, GOM)
+            for b in range(ROW):
+                row_sums = jnp.transpose(RK[b])[0:HEADS, :]
+                GDS[b] = dot(row_sums - CK[b] + U[b], MASK[b], HIGHEST)
         finish_b(k)
-    send_map(0, GIM, lambda b: dot_tn(WS[b].astype(BF16), MAP[1, b]))
+    part_of_map(0, GIM)
+    sum_of_map(0, GIM)
+    sum_of_map(1, GOM)
 
     for b in range(ROW):
-        row_sums = jnp.transpose(RK[b])[0:HEADS, :]
-        ck = CK[b]
         v = V[b]
-        GSS[b] = (ck + v) / STEP[b]
-        chain = dot(row_sums - ck + U[b], MASK[b], HIGHEST) + dot(v, PRE[b], HIGHEST)
-        GDS[b] = chain + HW[b] * TW[b] * B4[b]
+        GSS[b] = (CK[b] + v) / STEP[b]
+        GDS[b] += dot(v, PRE[b], HIGHEST) + HW[b] * TW[b] * B4[b]
     for dx in range(4):
         rows = pl.ds(pl.multiple_of(first_head, 16), 16)
         to_owner(GSS.at[chips[dx]], gs_out.at[rows], rs_one.at[R_GS], dx)

time: 57 us -> 55.1 us (0.967)
  Pallas kernels: 55.8 us -> 54.1 us
    pallas_call x1, Pallas kernels: 53.5 us -> 51.8 us  [per_device(): pl.pallas_call(kernel, out_shape=(jax.ShapeDtypeStruct((64 * W, T), BF16)...]
where the time goes in v5:
time: 55.1 us; the launch traced here: 54.9 us
  Pallas kernels  54.1 us (98%)
  between operations  0.8 us (1%)
    pallas_call x1, Pallas kernels, per_device(): pl.pallas_call(kernel, out_shape=(jax.ShapeDtypeStruct((64 * W, T), BF16)...  51.8 us
    pallas_call x1, Pallas kernels, per_device(): pl.pallas_call(settle, out_shape=(jax.ShapeDtypeStruct((64 * W, T), BF16)...  2.35 us

profile of v5, /device:TPU:1, one launch (start us, length us, event | category | flops | bytes accessed | tf_op | source)
XLA Modules:
  0.0 54.9 jit_solution(3374985446284432821)
XLA Ops:
  0.6 51.8 %ssd_backward.1 = (bf16[4096,128]{1,0:T(8,128)(2,1)}, f32[64,128]{1,0:T(8,128)}, f32[64,128]{1,0:T(8,128)}, bf16[2,2,128,256]{3,2,1,0:T(8,128)(2,1)}) custom-call(bf16[4096,128]{1,0:T(8,128)(2,1)} %bitcast.27, f32[64,128]{1,0:T(8,128)} %bitcast.31, f32[64,128]{1,0:T(8,128)} %bitcast.32, bf16[128,2,256]{2,1,0:T(2,128)(2,1)} %bitcast.29, ...), custom_call_target="tpu_custom_call" | custom-call | tf_op jit(solution)/shard_map/ssd_backward/pallas_call | solution.py:642
  52.4 2.4 %settle.1 = (bf16[4096,128]{1,0:T(8,128)(2,1)}, f32[64,128]{1,0:T(8,128)}, f32[64,128]{1,0:T(8,128)}, f32[128,2,256]{2,1,0:T(2,128)}, f32[128,2,256]{2,1,0:T(2,128)}) custom-call(bf16[4096,128]{1,0:T(8,128)(2,1)} %get-tuple-element.14.gf, f32[64,128]{1,0:T(8,128)} %get-tuple-element.15.gs, f32[64,128]{1,0:T(8,128)} %get-tuple-element.16.gd, ...), custom_call_target="tpu_custom_call" | custom-call | tf_op jit(solution)/shard_map/settle/pallas_call | solution.py:658

commit v6 on v5

--- a/solution.py
+++ b/solution.py
@@ -507,7 +507,6 @@
                 GDS[b] = dot(row_sums - CK[b] + U[b], MASK[b], HIGHEST)
         finish_b(k)
     part_of_map(0, GIM)
-    sum_of_map(0, GIM)
     sum_of_map(1, GOM)
 
     for b in range(ROW):
@@ -519,6 +518,7 @@
         to_owner(GSS.at[chips[dx]], gs_out.at[rows], rs_one.at[R_GS], dx)
         to_owner(GDS.at[chips[dx]], gd_out.at[rows], rs_one.at[R_GD], dx)
 
+    sum_of_map(0, GIM)
     arrived(PM, rs_one.at[R_PM])
     arrived(gf_out, rs_one.at[R_GF])
     arrived(gs_out, rs_one.at[R_GS])

time: 55.1 us -> 55.1 us (level)
  no operation moved by 1% of the time
where the time goes in v6:
time: 55.1 us; the launch traced here: 54.9 us
  Pallas kernels  54.1 us (98%)
  between operations  0.8 us (1%)
    pallas_call x1, Pallas kernels, per_device(): pl.pallas_call(kernel, out_shape=(jax.ShapeDtypeStruct((64 * W, T), BF16)...  51.8 us
    pallas_call x1, Pallas kernels, per_device(): pl.pallas_call(settle, out_shape=(jax.ShapeDtypeStruct((64 * W, T), BF16)...  2.35 us

profile of v6, /device:TPU:1, one launch (start us, length us, event | category | flops | bytes accessed | tf_op | source)
XLA Modules:
  0.0 54.9 jit_solution(7033838634901920903)
XLA Ops:
  0.6 51.8 %ssd_backward.1 = (bf16[4096,128]{1,0:T(8,128)(2,1)}, f32[64,128]{1,0:T(8,128)}, f32[64,128]{1,0:T(8,128)}, bf16[2,2,128,256]{3,2,1,0:T(8,128)(2,1)}) custom-call(bf16[4096,128]{1,0:T(8,128)(2,1)} %bitcast.27, f32[64,128]{1,0:T(8,128)} %bitcast.31, f32[64,128]{1,0:T(8,128)} %bitcast.32, bf16[128,2,256]{2,1,0:T(2,128)(2,1)} %bitcast.29, ...), custom_call_target="tpu_custom_call" | custom-call | tf_op jit(solution)/shard_map/ssd_backward/pallas_call | solution.py:642
  52.4 2.4 %settle.1 = (bf16[4096,128]{1,0:T(8,128)(2,1)}, f32[64,128]{1,0:T(8,128)}, f32[64,128]{1,0:T(8,128)}, f32[128,2,256]{2,1,0:T(2,128)}, f32[128,2,256]{2,1,0:T(2,128)}) custom-call(bf16[4096,128]{1,0:T(8,128)(2,1)} %get-tuple-element.14.gf, f32[64,128]{1,0:T(8,128)} %get-tuple-element.15.gs, f32[64,128]{1,0:T(8,128)} %get-tuple-element.16.gd, ...), custom_call_target="tpu_custom_call" | custom-call | tf_op jit(solution)/shard_map/settle/pallas_call | solution.py:658
